TPU v7x, 128 devices: a whole 4x4x4 slice. The times are simulated.
128 devices in a mesh: ctx: 32 (over x_lo, z, y), head: 4 (over x_hi, core).
Axes of the slice: x: 4 (x_hi: 2, x_lo: 2; x = x_hi * 2 + x_lo), y: 4, z: 4, core: 2. Of those that a mesh axis runs over, the one named last changes fastest.
Arguments:
- stretch_queries: bfloat16 [512, 128, 576], P('ctx', 'head'), may hold values from -500 to 500
- cache_latent: bfloat16 [8192, 576], P('ctx'), may hold values from -6 to 6
- doc_lengths: int32 [32], replicated, may hold values from 1 to 256, 6144 in all
- decode_queries: bfloat16 [128, 64, 576], P('ctx', 'head'), may hold values from -500 to 500
- w_attn_out: bfloat16 [64, 512, 7168], P('head', None, 'ctx'), may hold values from -0.25 to 0.25
- decode_hidden: bfloat16 [128, 7168], P('ctx'), may hold values from -6 to 6
- norm_gain: float32 [7168], replicated, may hold values from 0.1 to 1.9
- w_gate: bfloat16 [32, 7168, 2048], P('ctx', None, 'head'), may hold values from -0.0625 to 0.0625
- w_up: bfloat16 [32, 7168, 2048], P('ctx', None, 'head'), may hold values from -0.0625 to 0.0625
- w_down: bfloat16 [32, 2048, 7168], P('ctx', 'head'), may hold values from -0.125 to 0.125
- routes: int32 [3, 128, 8], P(None, 'ctx'), may hold values from 0 to 31, all different within a row; in each aligned block of 4 rows (0 to 3, 4 to 7, ..., all dimensions but the last counted through in order) at most 2 rows name the same one
- gate_weights: float32 [3, 128, 8], P(None, 'ctx'), may hold values from 0.05 to 0.4
Outputs:
- stretch_latent: bfloat16 [512, 128, 512], P('ctx', 'head')
- decode_out: bfloat16 [128, 7168], P('ctx')
Inputs may be any that keep to these rules, and one draw needn't show every extreme that they name: `routes`: in each step, among the 4 rows of one device, no expert is named by more than 2 rows, a bound that some block reaches; a row names 8 different experts. `doc_lengths`: every block has at least one used position and some block is full.
All inputs are finite; a program needn't handle non-finite values.
Results may differ from a plain program's by a relative error of at most 0.023.
Values may be sent and summed in bfloat16 or wider, within the bound.
No kernel may reach another device: no remote copies, remote signals or barrier semaphores. Data moves between devices by JAX's collectives and lax.ppermute only.
A program may use at most 128 MiB of HBM per device.

v0:
```python
import jax
import jax.numpy as jnp
from jax import lax
from jax.sharding import PartitionSpec as P

KV_RANK = 512
TOPK = 8
STEPS = 3


score_scale = 0.07216878364870322


def per_device(
    stretch_queries,
    cache_latent,
    doc_lengths,
    decode_queries,
    w_attn_out,
    decode_hidden,
    norm_gain,
    w_gate,
    w_up,
    w_down,
    routes,
    gate_weights,
):
    tok_count, head_count, full_width = stretch_queries.shape
    prefill_rows = tok_count * head_count
    row_local, dec_heads_local, _ = decode_queries.shape
    queries = jnp.concatenate(
        [
            stretch_queries.reshape(prefill_rows, full_width),
            decode_queries.reshape(row_local * dec_heads_local, full_width),
        ],
        axis=0,
    )
    row_total = queries.shape[0]
    block_len = cache_latent.shape[0]
    doc_count = doc_lengths.shape[0]
    piece = lax.all_gather(cache_latent, "ctx", axis=0, tiled=True)
    best_now = jnp.full((row_total,), -1e30, jnp.float32)
    scores = (
        lax.dot_general(
            queries, piece, (((1,), (1,)), ((), ())), preferred_element_type=jnp.float32
        )
        * score_scale
    )
    places = jnp.arange(piece.shape[0], dtype=jnp.int32)
    owners = places // block_len
    length_at = jnp.sum(
        jnp.where(
            owners[:, None] == jnp.arange(doc_count, dtype=jnp.int32)[None, :],
            doc_lengths[None, :],
            0,
        ),
        axis=1,
    )
    usable = places % block_len < length_at
    scores = jnp.where(usable[None, :], scores, -1e30)
    best_new = jnp.maximum(best_now, jnp.max(scores, axis=1))
    probs = jnp.where(usable[None, :], jnp.exp(scores - best_new[:, None]), 0.0)
    total_new = jnp.sum(probs, axis=1)
    acc_new = jnp.dot(
        probs.astype(jnp.bfloat16), piece[:, :KV_RANK], preferred_element_type=jnp.float32
    )
    latents = (acc_new / total_new[:, None]).astype(jnp.bfloat16)
    stretch_latent = latents[:prefill_rows].reshape(tok_count, head_count, KV_RANK)
    dec_latent = latents[prefill_rows:].reshape(row_local, dec_heads_local * KV_RANK)
    out_flat = w_attn_out.reshape(dec_heads_local * KV_RANK, w_attn_out.shape[2])
    partial_attn = jnp.dot(
        lax.all_gather(dec_latent, "ctx", axis=0, tiled=True),
        out_flat,
        preferred_element_type=jnp.float32,
    )
    attn_cols = lax.psum(partial_attn.astype(jnp.bfloat16), "head")
    attn_out = lax.all_to_all(attn_cols, "ctx", split_axis=0, concat_axis=1, tiled=True)
    state = (decode_hidden.astype(jnp.float32) + attn_out.astype(jnp.float32)).astype(jnp.bfloat16)
    ctx_size = lax.axis_size("ctx")
    local_experts = w_gate.shape[0]
    expert_total = ctx_size * local_experts
    slot_cap = max(2, 2 * row_local * TOPK // (ctx_size * local_experts))
    for step in range(STEPS):
        state_f = state.astype(jnp.float32)
        normed = (
            state_f
            * lax.rsqrt(jnp.mean(state_f * state_f, axis=1, keepdims=True) + 1e-06)
            * norm_gain
        ).astype(jnp.bfloat16)
        chosen = routes[step].reshape(-1)
        weights = gate_weights[step].reshape(-1)
        hits = (chosen[:, None] == jnp.arange(expert_total, dtype=jnp.int32)[None, :]).astype(
            jnp.int32
        )
        earlier = jnp.cumsum(hits, axis=0) - hits
        slot_of = jnp.sum(earlier * hits, axis=1)
        target = chosen * slot_cap + slot_of
        placed = (
            target[:, None] == jnp.arange(expert_total * slot_cap, dtype=jnp.int32)[None, :]
        ).astype(jnp.float32)
        dispatch_map = placed.reshape(row_local, TOPK, expert_total * slot_cap).sum(axis=1)
        combine_map = (
            (placed * weights[:, None])
            .reshape(row_local, TOPK, expert_total * slot_cap)
            .sum(axis=1)
        )
        outgoing = lax.dot_general(
            dispatch_map.astype(jnp.bfloat16),
            normed,
            (((0,), (0,)), ((), ())),
            preferred_element_type=jnp.float32,
        )
        outgoing = outgoing.astype(jnp.bfloat16).reshape(
            ctx_size, local_experts, slot_cap, normed.shape[1]
        )
        received = lax.all_to_all(outgoing, "ctx", split_axis=0, concat_axis=0, tiled=True)
        gate = jnp.einsum("sjcd,jdf->sjcf", received, w_gate, preferred_element_type=jnp.float32)
        upper = jnp.einsum("sjcd,jdf->sjcf", received, w_up, preferred_element_type=jnp.float32)
        inner = (jax.nn.silu(gate) * upper).astype(jnp.bfloat16)
        partial_out = jnp.einsum(
            "sjcf,jfd->sjcd", inner, w_down, preferred_element_type=jnp.float32
        )
        summed = lax.psum(partial_out.astype(jnp.bfloat16), "head")
        returned = lax.all_to_all(summed, "ctx", split_axis=0, concat_axis=0, tiled=True)
        returned = returned.reshape(expert_total * slot_cap, returned.shape[3]).astype(jnp.float32)
        added = jnp.dot(
            combine_map,
            returned,
            precision=lax.Precision.HIGHEST,
            preferred_element_type=jnp.float32,
        )
        state = (state_f + added).astype(jnp.bfloat16)
    return (stretch_latent, state)


def solution(mesh):
    return jax.shard_map(
        per_device,
        mesh=mesh,
        in_specs=(
            P("ctx", "head", None),
            P("ctx", None),
            P(),
            P("ctx", "head", None),
            P("head", None, "ctx"),
            P("ctx", None),
            P(),
            P("ctx", None, "head"),
            P("ctx", None, "head"),
            P("ctx", "head", None),
            P(None, "ctx", None),
            P(None, "ctx", None),
        ),
        out_specs=(P("ctx", "head", None), P("ctx", None)),
        check_vma=False,
    )
```

profile of v0, /device:TPU:1, one launch (start us, length us, event | category | flops | bytes accessed | tf_op | source)
XLA Modules:
  0.0 732.3 jit_solution(14406375090396949926)
XLA Ops:
  7.2 0.7 all-gather.4.cloned.1.call-update
  8.0 0.9 select_reduce_fusion
  8.9 163.4 %all-gather.4.cloned.1.call-done = bf16[8192,576]{0,1:T(8,128)(2,1)} async-done(((bf16[256,576]{0,1:T(8,128)(2,1)}), bf16[8192,576]{0,1:T(8,128)(2,1)}) %all-gather.4.cloned.1.call-update) | async-done | bytes 9437200 | tf_op jit(solution)/shard_map/all_gather | solution.py:41
  172.3 14.6 %fusion = (f32[576]{0:T(1024)S(1)}, f32[576,8192]{1,0:T(8,128)}) fusion(pred[8192]{0:T(1024)(128)(4,1)S(1)} %fusion.141, bf16[8192,576]{0,1:T(8,128)(2,1)} %all-gather.4.cloned.1.call-done, bf16[64,576]{1,0:T(8,128)(2,1)} %bitcast.212, bf16[512,576]{1,0:T(8,128)(2,1)} %bitcast.211), kind=kOutput, calls=%fused_computation.2 | convolution fusion | flops 5451300352 | bytes 28985600 | tf_op jit(solution)/shard_map/dot_general | solution.py:44
  186.9 11.7 %fusion.1 = f32[576]{0:T(1024)S(1)} fusion(f32[576,8192]{1,0:T(8,128)} %get-tuple-element.20, f32[576]{0:T(1024)S(1)} %broadcast_maximum_fusion, pred[8192]{0:T(1024)(128)(4,1)S(1)} %fusion.141), kind=kLoop, calls=%fused_computation.3 | loop fusion | flops 23592384 | bytes 18887168 | tf_op jit(solution)/shard_map/reduce_sum | solution.py:63
  198.6 11.8 %fusion.35 = bf16[576,512]{1,0:T(8,128)(2,1)S(1)} fusion(bf16[8192,576]{0,1:T(8,128)(2,1)} %all-gather.4.cloned.1.call-done, f32[576,8192]{1,0:T(8,128)} %get-tuple-element.20, f32[576]{0:T(1024)S(1)} %broadcast_maximum_fusion, pred[8192]{0:T(1024)(128)(4,1)S(1)} %fusion.141, f32[576]{0:T(1024)S(1)} %fusion.1), kind=kOutput, calls=%fused_computation.41 | convolution fusion | flops 4856020992 | bytes 27865600 | tf_op jit(solution)/shard_map/dot_general | solution.py:64
  210.4 0.7 reshape.274
  211.1 4.3 copy.51
  215.4 0.1 eq.108
  215.5 0.1 fusion.149
  215.6 0.2 select_reduce_fusion.6
  215.8 0.1 reduce_sum.135
  215.9 0.1 eq.115
  216.1 0.2 select_reduce_fusion.4
  216.3 0.1 reduce_sum.140
  216.4 0.1 eq.122
  216.6 0.2 select_reduce_fusion.2
  216.8 0.1 reduce_sum.145
  216.9 146.4 %all-gather.6.cloned.1.call-done = bf16[32,4,8192]{2,1,0:T(4,128)(2,1)} async-done(((bf16[1,4,8192]{2,1,0:T(4,128)(2,1)}), bf16[32,4,8192]{2,1,0:T(4,128)(2,1)}) %all-gather.6.cloned.1.call-update) | async-done | bytes 2097168 | tf_op jit(solution)/shard_map/all_gather | solution.py:72
  363.3 2.7 reshape.275
  366.0 3.1 convolution_convert_fusion.6
  369.2 0.1 copy.40
  369.3 35.3 %psum.28 = bf16[32,4,224]{2,1,0:T(4,128)(2,1)} all-reduce(bf16[32,4,224]{2,1,0:T(4,128)(2,1)S(1)} %all_to_all.28), channel_id=1, replica_groups=mesh['ctx'=32,'head'=4] {'head'}, use_global_device_ids=true, to_apply=%region_3.4 | all-reduce | flops 28672 | bytes 114688 | tf_op jit(solution)/shard_map/psum | solution.py:76
  404.6 6.7 all-to-all-start
  411.4 0.1 convert_reduce_fusion.2
  411.5 7.1 all-to-all-done
  418.6 0.2 reshape.273
  418.8 0.2 fusion.128
  419.0 0.5 convolution_convert_fusion.5
  419.4 0.3 reshape.258
  419.8 15.6 %all_to_all.43 = bf16[32,1,2,7168]{3,2,1,0:T(2,128)(2,1)S(1)} all-to-all(bf16[32,1,2,7168]{3,2,1,0:T(2,128)(2,1)S(1)} %bitcast.207), channel_id=1, replica_groups=mesh['ctx'=32,'head'=4] {'ctx'}, dimensions={0} | all-to-all | bytes 1835008 | tf_op jit(solution)/shard_map/all_to_all | solution.py:116
  435.4 4.5 fusion.40
  439.9 8.9 %fusion.7 = bf16[32,1,2,7168]{3,0,2,1:T(8,128)(2,1)} fusion(bf16[1,512,7168]{2,1,0:T(8,128)(2,1)} %param.21, bf16[1,7168,512]{2,1,0:T(8,128)(2,1)} %param.20, bf16[32,1,2,7168]{3,2,1,0:T(2,128)(2,1)S(1)} %all_to_all.43, f32[32,1,2,512]{3,0,2,1:T(8,128)S(1)} %fusion.40), kind=kOutput, calls=%fused_computation.14 | convolution fusion | flops 940179456 | bytes 16646144 | tf_op jit(solution)/shard_map/sjcf,jfd->sjcd/dot_general | solution.py:120
  448.8 46.2 %all-reduce.4.cloned.1.call-done = bf16[32,1,2,7168]{3,0,2,1:T(8,128)(2,1)} async-done(((bf16[32,1,2,7168]{3,0,2,1:T(8,128)(2,1)}), bf16[32,1,2,7168]{3,0,2,1:T(8,128)(2,1)}) %all-reduce.4.cloned.1.call-update) | async-done | bytes 917520 | tf_op jit(solution)/shard_map/psum | solution.py:123
  494.9 3.1 copy.44
  498.0 7.0 all-to-all-start.2
  505.1 0.1 convert_reduce_fusion.1
  505.2 13.9 %all-to-all-done.2 = bf16[32,1,2,7168]{3,2,1,0:T(2,128)(2,1)S(1)} async-done(((bf16[32,1,2,7168]{3,2,1,0:T(2,128)(2,1)}), bf16[32,1,2,7168]{3,2,1,0:T(2,128)(2,1)S(1)}, u32[]{:S(2)}, u32[]{:S(2)}) %all-to-all-start.2) | async-done | bytes 917536 | tf_op jit(solution)/shard_map/all_to_all | solution.py:124
  519.0 0.3 reshape.264
  519.4 0.6 multiply_reduce_fusion.1
  520.0 0.5 convolution_convert_fusion.4
  520.5 0.3 reshape.265
  520.8 18.9 %all_to_all.44 = bf16[32,1,2,7168]{3,2,1,0:T(2,128)(2,1)S(1)} all-to-all(bf16[32,1,2,7168]{3,2,1,0:T(2,128)(2,1)S(1)} %bitcast.208), channel_id=1, replica_groups=mesh['ctx'=32,'head'=4] {'ctx'}, dimensions={0} | all-to-all | bytes 1835008 | tf_op jit(solution)/shard_map/all_to_all | solution.py:116
  539.7 4.5 fusion.43
  544.2 8.9 %fusion.8 = bf16[32,1,2,7168]{3,0,2,1:T(8,128)(2,1)} fusion(bf16[1,512,7168]{2,1,0:T(8,128)(2,1)} %param.21, bf16[1,7168,512]{2,1,0:T(8,128)(2,1)} %param.20, bf16[32,1,2,7168]{3,2,1,0:T(2,128)(2,1)S(1)} %all_to_all.44, f32[32,1,2,512]{3,0,2,1:T(8,128)S(1)} %fusion.43), kind=kOutput, calls=%fused_computation.15 | convolution fusion | flops 940179456 | bytes 16646144 | tf_op jit(solution)/shard_map/sjcf,jfd->sjcd/dot_general | solution.py:120
  553.1 44.5 %all-reduce.6.cloned.1.call-done = bf16[32,1,2,7168]{3,0,2,1:T(8,128)(2,1)} async-done(((bf16[32,1,2,7168]{3,0,2,1:T(8,128)(2,1)}), bf16[32,1,2,7168]{3,0,2,1:T(8,128)(2,1)}) %all-reduce.6.cloned.1.call-update) | async-done | bytes 917520 | tf_op jit(solution)/shard_map/psum | solution.py:123
  597.6 3.1 copy.47
  600.7 7.0 all-to-all-start.4
  607.7 0.1 convert_reduce_fusion
  607.8 13.9 %all-to-all-done.4 = bf16[32,1,2,7168]{3,2,1,0:T(2,128)(2,1)S(1)} async-done(((bf16[32,1,2,7168]{3,2,1,0:T(2,128)(2,1)}), bf16[32,1,2,7168]{3,2,1,0:T(2,128)(2,1)S(1)}, u32[]{:S(2)}, u32[]{:S(2)}) %all-to-all-start.4) | async-done | bytes 917536 | tf_op jit(solution)/shard_map/all_to_all | solution.py:124
  621.7 0.3 reshape.268
  622.0 0.6 multiply_reduce_fusion
  622.6 0.5 convolution_convert_fusion.3
  623.1 0.3 reshape.269
  623.5 18.9 %all_to_all.45 = bf16[32,1,2,7168]{3,2,1,0:T(2,128)(2,1)S(1)} all-to-all(bf16[32,1,2,7168]{3,2,1,0:T(2,128)(2,1)S(1)} %bitcast.209), channel_id=1, replica_groups=mesh['ctx'=32,'head'=4] {'ctx'}, dimensions={0} | all-to-all | bytes 1835008 | tf_op jit(solution)/shard_map/all_to_all | solution.py:116
  642.4 4.5 fusion.46
  646.8 8.9 %fusion.9 = bf16[32,1,2,7168]{3,0,2,1:T(8,128)(2,1)} fusion(bf16[1,512,7168]{2,1,0:T(8,128)(2,1)} %param.21, bf16[1,7168,512]{2,1,0:T(8,128)(2,1)} %param.20, bf16[32,1,2,7168]{3,2,1,0:T(2,128)(2,1)S(1)} %all_to_all.45, f32[32,1,2,512]{3,0,2,1:T(8,128)S(1)} %fusion.46), kind=kOutput, calls=%fused_computation.16 | convolution fusion | flops 940179456 | bytes 16646144 | tf_op jit(solution)/shard_map/sjcf,jfd->sjcd/dot_general | solution.py:120
  655.7 44.5 %all-reduce.8.cloned.1.call-done = bf16[32,1,2,7168]{3,0,2,1:T(8,128)(2,1)} async-done(((bf16[32,1,2,7168]{3,0,2,1:T(8,128)(2,1)}), bf16[32,1,2,7168]{3,0,2,1:T(8,128)(2,1)}) %all-reduce.8.cloned.1.call-update) | async-done | bytes 917520 | tf_op jit(solution)/shard_map/psum | solution.py:123
  700.2 3.1 copy.50
  703.3 7.0 all-to-all-start.6
  710.3 0.8 slice.37
  711.1 13.2 %all-to-all-done.6 = bf16[32,1,2,7168]{3,2,1,0:T(2,128)(2,1)S(1)} async-done(((bf16[32,1,2,7168]{3,2,1,0:T(2,128)(2,1)}), bf16[32,1,2,7168]{3,2,1,0:T(2,128)(2,1)S(1)}, u32[]{:S(2)}, u32[]{:S(2)}) %all-to-all-start.6) | async-done | bytes 917536 | tf_op jit(solution)/shard_map/all_to_all | solution.py:124
  724.3 0.3 reshape.272
  724.7 1.1 fusion.14
  (35 shorter events, 0.8 us)
Async XLA Ops:
  7.2 165.1 %all-gather.4.cloned.1.call-start = ((), (), s32[]{:S(2)}) async-start(), calls=%async_computation.7 | async-start | bytes 9732096 | tf_op jit(solution)/shard_map/all_gather | solution.py:41
  7.9 355.4 %all-gather.6.cloned.1.call-start = ((), (), s32[]{:S(2)}) async-start(), calls=%async_computation.11 | async-start | bytes 2162688 | tf_op jit(solution)/shard_map/all_gather | solution.py:72
  210.3 5.0 copy-start.2
  210.4 6.5 copy-start.3
  215.4 203.4 %copy-start.1 = (bf16[4,7168]{1,0:T(4,128)(2,1)S(1)}, bf16[4,7168]{1,0:T(4,128)(2,1)}, u32[]{:S(2)}) copy-start(bf16[4,7168]{1,0:T(4,128)(2,1)} %param.17) | copy-start | bytes 172036
  215.4 203.6 %copy-start = (f32[7168]{0:T(1024)S(1)}, f32[7168]{0:T(1024)}, u32[]{:S(2)}) copy-start(f32[7168]{0:T(1024)} %param.18) | copy-start | bytes 86020
  404.6 13.9 %all-to-all-start = ((bf16[32,4,224]{2,1,0:T(4,128)(2,1)}), bf16[32,4,224]{2,1,0:T(4,128)(2,1)S(1)}, u32[]{:S(2)}, u32[]{:S(2)}) async-start(bf16[32,4,224]{2,1,0:T(4,128)(2,1)} %psum.28), calls=%async_computation | async-start | bytes 131072 | tf_op jit(solution)/shard_map/all_to_all | solution.py:77
  411.4 83.6 %all-reduce.4.cloned.1.call-start = ((), (), s32[]{:S(2)}) async-start(), calls=%async_computation.8 | async-start | bytes 1835008 | tf_op jit(solution)/shard_map/psum | solution.py:123
  498.0 21.0 %all-to-all-start.2 = ((bf16[32,1,2,7168]{3,2,1,0:T(2,128)(2,1)}), bf16[32,1,2,7168]{3,2,1,0:T(2,128)(2,1)S(1)}, u32[]{:S(2)}, u32[]{:S(2)}) async-start(bf16[32,1,2,7168]{3,2,1,0:T(2,128)(2,1)} %copy.44), calls=%async_computation.2 | async-start | bytes 1835008 | tf_op jit(solution)/shard_map/all_to_all | solution.py:124
  505.0 92.6 %all-reduce.6.cloned.1.call-start = ((), (), s32[]{:S(2)}) async-start(), calls=%async_computation.9 | async-start | bytes 1835008 | tf_op jit(solution)/shard_map/psum | solution.py:123
  600.7 21.0 %all-to-all-start.4 = ((bf16[32,1,2,7168]{3,2,1,0:T(2,128)(2,1)}), bf16[32,1,2,7168]{3,2,1,0:T(2,128)(2,1)S(1)}, u32[]{:S(2)}, u32[]{:S(2)}) async-start(bf16[32,1,2,7168]{3,2,1,0:T(2,128)(2,1)} %copy.47), calls=%async_computation.4 | async-start | bytes 1835008 | tf_op jit(solution)/shard_map/all_to_all | solution.py:124
  607.7 92.6 %all-reduce.8.cloned.1.call-start = ((), (), s32[]{:S(2)}) async-start(), calls=%async_computation.10 | async-start | bytes 1835008 | tf_op jit(solution)/shard_map/psum | solution.py:123
  703.3 21.0 %all-to-all-start.6 = ((bf16[32,1,2,7168]{3,2,1,0:T(2,128)(2,1)}), bf16[32,1,2,7168]{3,2,1,0:T(2,128)(2,1)S(1)}, u32[]{:S(2)}, u32[]{:S(2)}) async-start(bf16[32,1,2,7168]{3,2,1,0:T(2,128)(2,1)} %copy.50), calls=%async_computation.6 | async-start | bytes 1835008 | tf_op jit(solution)/shard_map/all_to_all | solution.py:124
Sparse Core Ops, SparseCore 0:
  9.6 162.6 all-gather.3
  211.2 152.0 all-gather.5
  448.9 45.9 all-reduce.3
  553.2 44.3 all-reduce.5
  655.9 44.3 all-reduce.7
where the time goes:
time: 734 us; the launch traced here: 732 us
  waiting for transfers between devices  494 us (67%)
  blocking collectives  88.7 us (12%)
  matrix products  73.3 us (10%)
  starting transfers between devices  27.9 us (4%)
  local copies, waits for them, and re-layouts  20.7 us (3%)
  other arithmetic  14 us (2%)
  between operations  14 us (2%)
    all_gather x1, waiting for transfers between devices, per_device(): piece = lax.all_gather(cache_latent, 'ctx', axis=0, tiled=True)  163 us
    all_gather x1, waiting for transfers between devices, per_device(): lax.all_gather(dec_latent, 'ctx', axis=0, tiled=True)  146 us
    psum x3, waiting for transfers between devices, per_device(): summed = lax.psum(partial_out.astype(jnp.bfloat16), 'head')  135 us
    all_to_all x3, blocking collectives, per_device(): lax.all_to_all(outgoing, 'ctx', split_axis=0, concat_axis=0, tiled=True)  53.4 us
    all_to_all x3, waiting for transfers between devices, per_device(): lax.all_to_all(summed, 'ctx', split_axis=0, concat_axis=0, tiled=True)  40.9 us
    psum x1, blocking collectives, per_device(): attn_cols = lax.psum(partial_attn.astype(jnp.bfloat16), 'head')  35.3 us
    dot_general x3, matrix products, per_device(): jnp.einsum('sjcf,jfd->sjcd', inner, w_down, preferred_element_type=jnp.fl...  26.7 us
    all_to_all x3, starting transfers between devices, per_device(): lax.all_to_all(summed, 'ctx', split_axis=0, concat_axis=0, tiled=True)  21 us
  transfers between devices with their start and end apart: 9, of which 9 were waited for; matrix products, arithmetic and copies ran while one was open for 1% of the time, Pallas kernels for 0%

commit v1 on v0

v1 whole, which is shorter than its diff:
```python
import functools

import jax
import jax.numpy as jnp
from jax import lax
from jax.experimental import pallas as pl
from jax.experimental.pallas import tpu as pltpu
from jax.sharding import Mesh, PartitionSpec as P

KV_RANK = 512
STEPS = 3
SLOTS = 2
SCALE = 0.07216878364870322
MASKED = -1e30

SPLIT = {"ctx": (("x_lo", 2), ("z", 4), ("y", 4)), "head": (("x_hi", 2), ("core", 2))}
CTX = ("x_lo", "z", "y")
HEAD = ("x_hi", "core")
SHARDS = ("x_lo", "z")
LANE = CTX + ("x_hi",)


def shift(x, axis, by):
    n = lax.axis_size(axis)
    return lax.ppermute(x, axis, [(i, (i + by) % n) for i in range(n)])


def spread(x, axes):
    n = lax.axis_size(axes)
    return lax.all_to_all(jnp.broadcast_to(x[None], (n,) + x.shape), axes, 0, 0, tiled=True)


def dot_t(a, b):
    return lax.dot_general(a, b, (((1,), (1,)), ((), ())), preferred_element_type=jnp.float32)


def dec_attn_kernel(q_ref, kv_ref, bias_ref, out_ref):
    kv = kv_ref[...]
    s = dot_t(q_ref[...], kv) * SCALE + bias_ref[...]
    top = jnp.max(s, axis=1, keepdims=True)
    p = jnp.exp(s - top)
    total = jnp.sum(p, axis=1, keepdims=True)
    acc = jnp.dot(p.astype(jnp.bfloat16), kv[:, :KV_RANK], preferred_element_type=jnp.float32)
    out_ref[:, :KV_RANK] = (acc / total).astype(jnp.bfloat16)
    lse = jnp.broadcast_to(top + jnp.log(total), (q_ref.shape[0], 128))
    hi = lse.astype(jnp.bfloat16).astype(jnp.float32)
    mid = (lse - hi).astype(jnp.bfloat16).astype(jnp.float32)
    low = lse - hi - mid
    lane = lax.broadcasted_iota(jnp.int32, lse.shape, 1)
    out_ref[:, KV_RANK:] = jnp.where(
        lane == 0, hi, jnp.where(lane == 1, mid, jnp.where(lane == 2, low, 0.0))
    ).astype(jnp.bfloat16)


def combine_kernel(parts_ref, out_ref):
    n = parts_ref.shape[0]
    lses = [
        jnp.sum(parts_ref[i, :, KV_RANK:].astype(jnp.float32), axis=1, keepdims=True)
        for i in range(n)
    ]
    top = functools.reduce(jnp.maximum, lses)
    shares = [jnp.exp(x - top) for x in lses]
    total = functools.reduce(jnp.add, shares)
    acc = sum(shares[i] * parts_ref[i, :, :KV_RANK].astype(jnp.float32) for i in range(n))
    out_ref[...] = (acc / total).astype(jnp.bfloat16)


def prefill_kernel(q_ref, kv_a, kv_b, bias_a, bias_b, out_ref, top_ref, total_ref, acc_ref):
    step = pl.program_id(0)

    @pl.when(step == 0)
    def _():
        top_ref[...] = jnp.full_like(top_ref, MASKED)
        total_ref[...] = jnp.zeros_like(total_ref)
        acc_ref[...] = jnp.zeros_like(acc_ref)

    q = q_ref[...]
    for kv_ref, bias_ref in ((kv_a, bias_a), (kv_b, bias_b)):
        kv = kv_ref[...]
        s = dot_t(q, kv) * SCALE + bias_ref[...]
        old = top_ref[...]
        top = jnp.maximum(old, jnp.max(s, axis=1, keepdims=True))
        p = jnp.exp(s - top)
        fade = jnp.exp(old - top)
        total_ref[...] = total_ref[...] * fade + jnp.sum(p, axis=1, keepdims=True)
        acc_ref[...] = acc_ref[...] * fade + jnp.dot(
            p.astype(jnp.bfloat16), kv[:, :KV_RANK], preferred_element_type=jnp.float32
        )
        top_ref[...] = top

    @pl.when(step == pl.num_programs(0) - 1)
    def _():
        out_ref[...] = (acc_ref[...] / total_ref[...]).astype(jnp.bfloat16)


def prefill(q, kv_a, kv_b, bias_a, bias_b):
    rows, width = q.shape
    count = kv_a.shape[0]
    block = 1024
    kv_spec = pl.BlockSpec((block, width), lambda i: (i, 0))
    bias_spec = pl.BlockSpec((1, block), lambda i: (0, i))
    return pl.pallas_call(
        prefill_kernel,
        grid=(count // block,),
        in_specs=[pl.BlockSpec((rows, width), lambda i: (0, 0)), kv_spec, kv_spec, bias_spec, bias_spec],
        out_specs=pl.BlockSpec((rows, KV_RANK), lambda i: (0, 0)),
        out_shape=jax.ShapeDtypeStruct((rows, KV_RANK), jnp.bfloat16),
        scratch_shapes=[
            pltpu.VMEM((rows, 1), jnp.float32),
            pltpu.VMEM((rows, 1), jnp.float32),
            pltpu.VMEM((rows, KV_RANK), jnp.float32),
        ],
        compiler_params=pltpu.CompilerParams(vmem_limit_bytes=40 << 20),
        cost_estimate=pl.CostEstimate(
            flops=2 * rows * 2 * count * (width + KV_RANK),
            bytes_accessed=4 * count * width,
            transcendentals=2 * rows * count,
        ),
        name="prefill",
    )(q, kv_a, kv_b, bias_a, bias_b)


def inner_kernel(x_ref, gain_ref, gate_ref, up_ref, out_ref, x_scr, gate_acc, up_acc):
    step = pl.program_id(0)
    chunk = gate_ref.shape[0]

    @pl.when(step == 0)
    def _():
        halves = x_ref.shape[0]
        width = x_ref.shape[2]
        xs = [x_ref[i].astype(jnp.float32) for i in range(halves)]
        square = sum(jnp.sum(x * x, axis=1, keepdims=True) for x in xs) / (halves * width)
        scale = lax.rsqrt(square + 1e-06)
        for i in range(halves):
            x = (xs[i] * scale * gain_ref[:, i * width : (i + 1) * width]).astype(jnp.bfloat16)
            for j in range(width // chunk):
                x_scr[i * (width // chunk) + j] = x[:, j * chunk : (j + 1) * chunk]
        gate_acc[...] = jnp.zeros_like(gate_acc)
        up_acc[...] = jnp.zeros_like(up_acc)

    x = x_scr[step]
    gate_acc[...] += jnp.dot(x, gate_ref[...], preferred_element_type=jnp.float32)
    up_acc[...] += jnp.dot(x, up_ref[...], preferred_element_type=jnp.float32)

    @pl.when(step == pl.num_programs(0) - 1)
    def _():
        out_ref[...] = (jax.nn.silu(gate_acc[...]) * up_acc[...]).astype(jnp.bfloat16)


def expert_inner(x, gain, w_gate, w_up):
    halves, rows, width = x.shape
    depth, hidden = w_gate.shape
    chunk = 896
    w_spec = pl.BlockSpec((chunk, hidden), lambda i: (i, 0))
    return pl.pallas_call(
        inner_kernel,
        grid=(depth // chunk,),
        in_specs=[
            pl.BlockSpec(x.shape, lambda i: (0, 0, 0)),
            pl.BlockSpec((1, depth), lambda i: (0, 0)),
            w_spec,
            w_spec,
        ],
        out_specs=pl.BlockSpec((rows, hidden), lambda i: (0, 0)),
        out_shape=jax.ShapeDtypeStruct((rows, hidden), jnp.bfloat16),
        scratch_shapes=[
            pltpu.VMEM((depth // chunk, rows, chunk), jnp.bfloat16),
            pltpu.VMEM((rows, hidden), jnp.float32),
            pltpu.VMEM((rows, hidden), jnp.float32),
        ],
        compiler_params=pltpu.CompilerParams(vmem_limit_bytes=24 << 20),
        cost_estimate=pl.CostEstimate(
            flops=4 * rows * depth * hidden, bytes_accessed=4 * depth * hidden, transcendentals=rows * hidden
        ),
        name="expert_inner",
    )(x, gain, w_gate, w_up)


def down_kernel(core_ref, inner_ref, own_ref, other_ref, out_ref):
    core = core_ref[0]
    out_ref[...] = (
        jnp.dot(inner_ref[core], own_ref[...], preferred_element_type=jnp.float32)
        + jnp.dot(inner_ref[1 - core], other_ref[...], preferred_element_type=jnp.float32)
    ).astype(jnp.bfloat16)


def expert_down(core, inner, w_down, w_other):
    cores, rows, hidden = inner.shape
    width = w_other.shape[1]
    block = 896
    steps = width // block
    return pl.pallas_call(
        down_kernel,
        grid_spec=pltpu.PrefetchScalarGridSpec(
            num_scalar_prefetch=1,
            grid=(steps,),
            in_specs=[
                pl.BlockSpec(inner.shape, lambda i, core: (0, 0, 0)),
                pl.BlockSpec((hidden, block), lambda i, core: (0, core[0] * steps + i)),
                pl.BlockSpec((hidden, block), lambda i, core: (0, i)),
            ],
            out_specs=pl.BlockSpec((rows, block), lambda i, core: (0, i)),
        ),
        out_shape=jax.ShapeDtypeStruct((rows, width), jnp.bfloat16),
        compiler_params=pltpu.CompilerParams(vmem_limit_bytes=24 << 20),
        cost_estimate=pl.CostEstimate(
            flops=4 * rows * hidden * width, bytes_accessed=4 * hidden * width, transcendentals=0
        ),
        name="expert_down",
    )(core, inner, w_down, w_other)


def per_device(
    stretch_queries,
    cache_latent,
    doc_lengths,
    decode_queries,
    w_attn_out,
    decode_hidden,
    norm_gain,
    w_gate,
    w_up,
    w_down,
    routes,
    gate_weights,
):
    tokens, heads, width = stretch_queries.shape
    rows, dec_heads, _ = decode_queries.shape
    block = cache_latent.shape[0]
    half = block // 2
    ctx_size = lax.axis_size(CTX)
    model = decode_hidden.shape[1]
    core = lax.axis_index("core")
    x_hi = lax.axis_index("x_hi")
    quarter = model // 4
    my_quarter = core * 2 + x_hi

    mine = lax.dynamic_slice_in_dim(cache_latent, core * half, half, 0)

    line = jnp.stack([mine] + [shift(mine, "y", by) for by in (1, 3, 2)])
    dec_q = decode_queries.reshape(rows * dec_heads, width)
    group_q = spread(dec_q, SHARDS)
    shards = group_q.shape[0]
    line_kv = lax.all_gather(line, "core", axis=0)
    y = lax.axis_index("y")
    line_at = lax.axis_index(SHARDS) * 4 + (y - jnp.array([0, 1, 3, 2], jnp.int32)) % 4
    place = jnp.arange(block, dtype=jnp.int32).reshape(2, 1, half)
    line_bias = jnp.where(place < doc_lengths[line_at][None, :, None], 0.0, MASKED).astype(jnp.float32)
    group_rows = shards * rows * dec_heads
    parts = pl.pallas_call(
        dec_attn_kernel,
        out_shape=jax.ShapeDtypeStruct((group_rows, KV_RANK + 128), jnp.bfloat16),
        compiler_params=pltpu.CompilerParams(vmem_limit_bytes=40 << 20),
        name="decode_attention",
    )(
        group_q.reshape(group_rows, width),
        line_kv.reshape(4 * block, width),
        line_bias.reshape(1, 4 * block),
    )
    parts = lax.all_to_all(
        parts.reshape(shards, rows * dec_heads, KV_RANK + 128), SHARDS, 0, 0, tiled=True
    )
    dec_latent = pl.pallas_call(
        combine_kernel,
        out_shape=jax.ShapeDtypeStruct((rows * dec_heads, KV_RANK), jnp.bfloat16),
        name="combine_shards",
    )(parts)

    all_latent = spread(dec_latent, CTX).reshape(ctx_size * rows, dec_heads * KV_RANK)
    cols = w_attn_out.shape[2]
    partial_attn = jnp.dot(
        all_latent, w_attn_out.reshape(dec_heads * KV_RANK, cols), preferred_element_type=jnp.float32
    ).astype(jnp.bfloat16)
    partial_attn = jnp.broadcast_to(
        partial_attn.reshape(ctx_size, 1, rows, cols), (ctx_size, 4, rows, cols)
    ).reshape(ctx_size * 4, rows, cols)
    partial_attn = lax.all_to_all(partial_attn, CTX + HEAD, 0, 0, tiled=True)
    partial_attn = partial_attn.reshape(ctx_size, 4, rows, cols)
    partial_attn = lax.dynamic_slice_in_dim(partial_attn, my_quarter * (ctx_size // 4), ctx_size // 4, 0)
    attn_out = jnp.sum(partial_attn.astype(jnp.float32), axis=1).astype(jnp.bfloat16)
    attn_out = jnp.swapaxes(attn_out, 0, 1).reshape(rows, quarter)
    hidden_quarter = lax.dynamic_slice_in_dim(decode_hidden, my_quarter * quarter, quarter, 1)
    state = (hidden_quarter.astype(jnp.float32) + attn_out.astype(jnp.float32)).astype(jnp.bfloat16)

    experts = jnp.arange(ctx_size, dtype=jnp.int32)
    hits = routes[..., None] == experts
    used = jnp.any(hits, axis=2)
    weight = jnp.sum(jnp.where(hits, gate_weights[..., None], 0.0), axis=2)
    counted = used.astype(jnp.int32)
    earlier = jnp.cumsum(counted, axis=1) - counted
    placed = used[..., None] & (earlier[..., None] == jnp.arange(SLOTS, dtype=jnp.int32))
    dispatch = jnp.moveaxis(placed, 1, -1).astype(jnp.bfloat16)
    dispatch = dispatch.reshape(STEPS, ctx_size * SLOTS, rows)
    collect = jnp.where(placed, weight[..., None], 0.0)
    collect = jnp.broadcast_to(collect[:, :, :, None, :], (STEPS, rows, ctx_size, 2, SLOTS))
    collect = collect.reshape(STEPS, rows, ctx_size * 2 * SLOTS)

    other_cols = lax.dynamic_slice_in_dim(w_down[0], (1 - core) * (model // 2), model // 2, 1)
    w_other = shift(other_cols, "core", 1)
    core_arr = core.astype(jnp.int32).reshape(1)
    gain = norm_gain.reshape(1, model)

    for step in range(STEPS):
        outgoing = jnp.dot(dispatch[step], state, preferred_element_type=jnp.float32)
        outgoing = outgoing.astype(jnp.bfloat16).reshape(ctx_size, 1, SLOTS, quarter)
        outgoing = jnp.broadcast_to(outgoing, (ctx_size, 2, SLOTS, quarter))
        received = lax.all_to_all(
            outgoing.reshape(ctx_size * 2, SLOTS, quarter), LANE, 0, 0, tiled=True
        )
        received = received.reshape(ctx_size, 2, SLOTS, quarter)
        received = jnp.swapaxes(received, 1, 2).reshape(ctx_size * SLOTS, 2 * quarter)
        received = lax.all_gather(received, "core", axis=0)
        inner = expert_inner(received, gain, w_gate[0], w_up[0])
        inner = lax.all_gather(inner, "core", axis=0)
        partial_out = expert_down(core_arr, inner, w_down[0], w_other)
        partial_out = partial_out.reshape(ctx_size, SLOTS, 2, quarter)
        partial_out = jnp.swapaxes(partial_out, 1, 2).reshape(ctx_size * 2, SLOTS, quarter)
        returned = lax.all_to_all(partial_out, LANE, 0, 0, tiled=True)
        returned = returned.reshape(ctx_size * 2 * SLOTS, quarter).astype(jnp.float32)
        added = jnp.dot(
            collect[step], returned, precision=lax.Precision.HIGHEST, preferred_element_type=jnp.float32
        )
        state = (state.astype(jnp.float32) + added).astype(jnp.bfloat16)
    decode_out = lax.all_gather(state, HEAD, axis=0)
    decode_out = decode_out.reshape(2, 2, rows, quarter).transpose(2, 1, 0, 3).reshape(rows, model)

    gathered = lax.all_gather(mine, CTX, axis=0)
    others = shift(gathered, "core", 1)
    at = jnp.arange(half, dtype=jnp.int32)[None, :]

    def bias_of(which):
        return jnp.where(at + which * half < doc_lengths[:, None], 0.0, MASKED).astype(jnp.float32)

    stretch_latent = prefill(
        stretch_queries.reshape(tokens * heads, width),
        gathered.reshape(ctx_size * half, width),
        others.reshape(ctx_size * half, width),
        bias_of(core).reshape(1, ctx_size * half),
        bias_of(1 - core).reshape(1, ctx_size * half),
    )
    return stretch_latent.reshape(tokens, heads, KV_RANK), decode_out


def solution(mesh):
    names = [name for axis in mesh.axis_names for name, _ in SPLIT[axis]]
    sizes = [size for axis in mesh.axis_names for _, size in SPLIT[axis]]
    fine = Mesh(mesh.devices.reshape(sizes), names)
    return jax.shard_map(
        per_device,
        mesh=fine,
        in_specs=(
            P(CTX, HEAD, None),
            P(CTX, None),
            P(),
            P(CTX, HEAD, None),
            P(HEAD, None, CTX),
            P(CTX, None),
            P(),
            P(CTX, None, HEAD),
            P(CTX, None, HEAD),
            P(CTX, HEAD, None),
            P(None, CTX, None),
            P(None, CTX, None),
        ),
        out_specs=(P(CTX, HEAD, None), P(CTX, None)),
        check_vma=False,
    )
```

time: 734 us -> 425 us (0.58)
  waiting for transfers between devices: 494 us -> 142 us
  matrix products: 73.3 us -> 5.64 us
  Pallas kernels: 0 us -> 46.3 us
  local copies, waits for them, and re-layouts: 20.7 us -> 66.1 us
  starting transfers between devices: 27.9 us -> 66.9 us
  other arithmetic: 14 us -> 1.61 us
  blocking collectives: 88.7 us -> 80.6 us
    all_gather x2, waiting for transfers between devices: 310 us -> 55.7 us  [the longest x1 52 us: per_device(): gathered = lax.all_gather(mine, CTX, axis=0)]
    psum x3 -> x0, waiting for transfers between devices: 135 us -> none  [per_device(): summed = lax.psum(partial_out.astype(jnp.bfloat16), 'head')]
    dot_general x15 -> x7, matrix products: 73.3 us -> 5.64 us  [the longest x1 3.78 us: per_device(): jnp.dot(all_latent, w_attn_out.reshape(dec_heads * KV_RANK, cols), prefer...]
    pallas_call x0 -> x9, Pallas kernels: none -> 46.3 us  [the longest x1 17.9 us: prefill(): pl.pallas_call(prefill_kernel, grid=(count // block,), in_specs=[pl.Block...]
    psum x1 -> x0, blocking collectives: 35.3 us -> none  [per_device(): attn_cols = lax.psum(partial_attn.astype(jnp.bfloat16), 'head')]
    all_gather x0 -> x7, blocking collectives: none -> 31.7 us  [the longest x3 17.4 us: per_device(): received = lax.all_gather(received, 'core', axis=0)]
    all_to_all x4 -> x7, waiting for transfers between devices: 48 us -> 75 us  [the longest x3 34.7 us: per_device(): returned = lax.all_to_all(partial_out, LANE, 0, 0, tiled=True)]
    ppermute x0 -> x5, starting transfers between devices: none -> 26.5 us  [shift(): return lax.ppermute(x, axis, [(i, (i + by) % n) for i in range(n)])]
  transfers between devices with their start and end apart: 9 -> 14, of which waited for: 9 -> 10; matrix products, arithmetic and copies ran while one was open for 1% -> 9% of each run, Pallas kernels for 0% -> 7%
where the time goes in v1:
time: 425 us; the launch traced here: 423 us
  waiting for transfers between devices  142 us (33%)
  blocking collectives  80.6 us (19%)
  starting transfers between devices  66.9 us (16%)
  local copies, waits for them, and re-layouts  66.1 us (16%)
  Pallas kernels  46.3 us (11%)
  between operations  14.6 us (3%)
  matrix products  5.64 us (1%)
    all_gather x1, waiting for transfers between devices, per_device(): gathered = lax.all_gather(mine, CTX, axis=0)  52 us
    all_to_all x3, waiting for transfers between devices, per_device(): returned = lax.all_to_all(partial_out, LANE, 0, 0, tiled=True)  34.7 us
    all_to_all x2, blocking collectives, per_device(): lax.all_to_all(outgoing.reshape(ctx_size * 2, SLOTS, quarter), LANE, 0, 0...  30 us
    all_to_all x2, waiting for transfers between devices, spread(): lax.all_to_all(jnp.broadcast_to(x[None], (n,) + x.shape), axes, 0, 0, til...  28.4 us
    ppermute x5, starting transfers between devices, shift(): return lax.ppermute(x, axis, [(i, (i + by) % n) for i in range(n)])  26.5 us
    unnamed x51, local copies, waits for them, and re-layouts  24.9 us
    all_to_all x1, blocking collectives, per_device(): lax.all_to_all(parts.reshape(shards, rows * dec_heads, KV_RANK + 128), SH...  19 us
    pallas_call x1, Pallas kernels, prefill(): pl.pallas_call(prefill_kernel, grid=(count // block,), in_specs=[pl.Block...  17.9 us
  transfers between devices with their start and end apart: 14, of which 10 were waited for; matrix products, arithmetic and copies ran while one was open for 9% of the time, Pallas kernels for 7%

profile of v1, /device:TPU:1, one launch (start us, length us, event | category | flops | bytes accessed | tf_op | source)
XLA Modules:
  0.0 423.2 jit_solution(3207362006390575768)
XLA Ops:
  7.3 0.9 copy-done
  8.4 3.6 collective-permute-start.2
  13.0 5.4 %collective-permute-done.2 = bf16[128,576]{1,0:T(8,128)(2,1)S(1)} collective-permute-done((bf16[128,576]{1,0:T(8,128)(2,1)S(1)}, bf16[128,576]{1,0:T(8,128)(2,1)S(1)}, u32[]{:S(2)}, u32[]{:S(2)}) %collective-permute-start.2) | collective-permute-done | bytes 147488 | tf_op jit(solution)/shard_map/ppermute | solution.py:25
  18.4 4.7 %collective-permute-done.1 = bf16[128,576]{1,0:T(8,128)(2,1)S(1)} collective-permute-done((bf16[128,576]{1,0:T(8,128)(2,1)S(1)}, bf16[128,576]{1,0:T(8,128)(2,1)S(1)}, u32[]{:S(2)}, u32[]{:S(2)}) %collective-permute-start.1) | collective-permute-done | bytes 147488 | tf_op jit(solution)/shard_map/ppermute | solution.py:25
  23.3 1.0 copy.81
  25.1 0.9 broadcast_in_dim.116
  26.0 6.0 %all-to-all-start = ((bf16[8,64,576]{2,1,0:T(8,128)(2,1)}), bf16[8,64,576]{2,1,0:T(8,128)(2,1)S(1)}, u32[]{:S(2)}, u32[]{:S(2)}) async-start(bf16[8,64,576]{2,1,0:T(8,128)(2,1)} %broadcast_in_dim.116), calls=%async_computation | async-start | bytes 1310720 | tf_op jit(solution)/shard_map/all_to_all | solution.py:30
  32.8 3.7 all-gather.12.cloned.1.call-done
  36.5 1.7 copy.82
  38.2 3.4 all-to-all-done
  41.6 1.9 decode_attention.1
  43.5 19.0 %all_to_all.50.parts_ref = bf16[8,64,640]{2,1,0:T(8,128)(2,1)} all-to-all(bf16[8,64,640]{2,1,0:T(8,128)(2,1)S(1)} %bitcast.115), channel_id=1, replica_groups=mesh['x_lo'=2,'z'=4,'y'=4,'x_hi'=2,'core'=2] {'x_lo','z'}, dimensions={0} | all-to-all | bytes 1310720 | tf_op jit(solution)/shard_map/all_to_all | solution.py:260
  62.5 2.0 combine_shards.1
  64.5 2.4 broadcast_in_dim.120
  66.8 6.1 %all-to-all-start.2 = ((bf16[32,64,512]{2,1,0:T(8,128)(2,1)}), bf16[32,64,512]{2,1,0:T(8,128)(2,1)S(1)}, u32[]{:S(2)}, u32[]{:S(2)}) async-start(bf16[32,64,512]{2,1,0:T(8,128)(2,1)} %broadcast_in_dim.120), calls=%async_computation.2 | async-start | bytes 4194304 | tf_op jit(solution)/shard_map/all_to_all | solution.py:30
  73.0 4.3 %dynamic-slice_bitcast_fusion = bf16[512,3584]{1,0:T(8,128)(2,1)} fusion(bf16[1,512,7168]{2,1,0:T(8,128)(2,1)} %param.22, s32[]{:T(128)S(6)} %select_n.91), kind=kLoop, calls=%fused_computation.1 | loop fusion | bytes 7340036 | tf_op jit(solution)/shard_map/dynamic_slice | solution.py:298
  77.4 1.9 collective-permute-start.4
  79.3 2.2 copy.98
  81.6 25.0 %all-to-all-done.2 = bf16[32,64,512]{2,1,0:T(8,128)(2,1)S(1)} async-done(((bf16[32,64,512]{2,1,0:T(8,128)(2,1)}), bf16[32,64,512]{2,1,0:T(8,128)(2,1)S(1)}, u32[]{:S(2)}, u32[]{:S(2)}) %all-to-all-start.2) | async-done | bytes 2097184 | tf_op jit(solution)/shard_map/all_to_all | solution.py:30
  106.7 2.3 reshape.291
  109.0 3.8 convolution_convert_fusion.3
  112.9 0.8 broadcast_in_dim.122
  113.7 9.1 %all-to-all-start.3 = ((bf16[128,4,224]{2,1,0:T(4,128)(2,1)}), bf16[128,4,224]{2,1,0:T(4,128)(2,1)S(1)}, u32[]{:S(2)}, u32[]{:S(2)}) async-start(bf16[128,4,224]{2,1,0:T(4,128)(2,1)} %bitcast.15), calls=%async_computation.3 | async-start | bytes 524288 | tf_op jit(solution)/shard_map/all_to_all | solution.py:277
  123.1 11.9 %all-to-all-done.3 = bf16[128,4,224]{2,1,0:T(4,128)(2,1)S(1)} async-done(((bf16[128,4,224]{2,1,0:T(4,128)(2,1)}), bf16[128,4,224]{2,1,0:T(4,128)(2,1)S(1)}, u32[]{:S(2)}, u32[]{:S(2)}) %all-to-all-start.3) | async-done | bytes 229408 | tf_op jit(solution)/shard_map/all_to_all | solution.py:277
  135.2 0.7 add_convert_fusion
  136.3 1.0 broadcast_in_dim.130
  137.3 4.6 %all-to-all-start.4 = ((bf16[64,2,1792]{2,1,0:T(2,128)(2,1)}), bf16[64,2,1792]{2,1,0:T(2,128)(2,1)S(1)}, u32[]{:S(2)}, u32[]{:S(2)}) async-start(bf16[64,2,1792]{2,1,0:T(2,128)(2,1)} %bitcast.23), calls=%async_computation.4 | async-start | bytes 917504 | tf_op jit(solution)/shard_map/all_to_all | solution.py:307
  141.9 52.0 %all-gather.10.cloned.1.call-done.kv_a = bf16[4096,576]{1,0:T(8,128)(2,1)} async-done(((bf16[128,576]{1,0:T(8,128)(2,1)}), bf16[4096,576]{1,0:T(8,128)(2,1)}) %all-gather.10.cloned.1.call-update) | async-done | bytes 4718608 | tf_op jit(solution)/shard_map/all_gather | solution.py:327
  193.9 7.6 %copy.79 = bf16[32,128,576]{1,2,0:T(8,128)(2,1)} copy(bf16[32,128,576]{2,1,0:T(8,128)(2,1)} %bitcast.111) | data formatting | bytes 9437184 | tf_op jit(solution)/shard_map/all_gather | solution.py:327
  201.5 19.9 %collective-permute-start = (bf16[32,128,576]{1,2,0:T(8,128)(2,1)}, bf16[32,128,576]{1,2,0:T(8,128)(2,1)}, u32[]{:S(2)}, u32[]{:S(2)}) collective-permute-start(bf16[32,128,576]{1,2,0:T(8,128)(2,1)} %copy.79), channel_id=1, source_target_pairs={{0,1},{1,0},{2,3},{3,2},{4,5},{5,4},{6,7},{7,6},{8,9},{9,8},{10,11... | collective-permute-start | bytes 14155784 | tf_op jit(solution)/shard_map/ppermute | solution.py:25
  222.6 7.0 %all_gather.49.x_ref = bf16[2,64,3584]{2,1,0:T(8,128)(2,1)S(1)} all-gather(bf16[1,64,3584]{2,1,0:T(8,128)(2,1)S(1)} %all_gather_reshape.9), channel_id=1, replica_groups=mesh['x_lo'=2,'z'=4,'y'=4,'x_hi'=2,'core'=2] {'core'}, dimensions={0}, use_global_device_ids=true | all-gather | bytes 1376256 | tf_op jit(solution)/shard_map/all_gather | solution.py:312
  229.5 3.2 copy-done.2
  232.8 3.2 copy-done.5
  236.0 4.1 expert_inner.3
  240.1 2.1 all-gather.2
  242.2 4.1 expert_down.3
  246.4 1.1 copy.90
  247.5 5.0 %all-to-all-start.5 = ((bf16[64,2,1792]{2,1,0:T(2,128)(2,1)}), bf16[64,2,1792]{2,1,0:T(2,128)(2,1)S(1)}, u32[]{:S(2)}, u32[]{:S(2)}) async-start(bf16[64,2,1792]{2,1,0:T(2,128)(2,1)} %bitcast.33), calls=%async_computation.5 | async-start | bytes 917504 | tf_op jit(solution)/shard_map/all_to_all | solution.py:318
  252.7 11.4 %all-to-all-done.5 = bf16[64,2,1792]{2,1,0:T(2,128)(2,1)S(1)} async-done(((bf16[64,2,1792]{2,1,0:T(2,128)(2,1)}), bf16[64,2,1792]{2,1,0:T(2,128)(2,1)S(1)}, u32[]{:S(2)}, u32[]{:S(2)}) %all-to-all-start.5) | async-done | bytes 458784 | tf_op jit(solution)/shard_map/all_to_all | solution.py:318
  265.2 15.0 %all_to_all.51 = bf16[64,2,1792]{2,1,0:T(2,128)(2,1)S(1)} all-to-all(bf16[64,2,1792]{2,1,0:T(2,128)(2,1)S(1)} %bitcast.131), channel_id=1, replica_groups=mesh['x_lo'=2,'z'=4,'y'=4,'x_hi'=2,'core'=2] {'x_lo','z','y','x_hi'}, dimensions={0} | all-to-all | bytes 917504 | tf_op jit(solution)/shard_map/all_to_all | solution.py:307
  280.9 5.3 %all_gather.52.x_ref = bf16[2,64,3584]{2,1,0:T(8,128)(2,1)S(1)} all-gather(bf16[1,64,3584]{2,1,0:T(8,128)(2,1)S(1)} %all_gather_reshape.10), channel_id=1, replica_groups=mesh['x_lo'=2,'z'=4,'y'=4,'x_hi'=2,'core'=2] {'core'}, dimensions={0}, use_global_device_ids=true | all-gather | bytes 1376256 | tf_op jit(solution)/shard_map/all_gather | solution.py:312
  286.2 3.1 copy-done.3
  289.3 3.1 copy-done.6
  292.3 4.1 expert_inner.4
  296.4 1.9 all-gather.3
  298.4 4.1 expert_down.4
  302.6 1.1 copy.92
  303.7 4.6 %all-to-all-start.7 = ((bf16[64,2,1792]{2,1,0:T(2,128)(2,1)}), bf16[64,2,1792]{2,1,0:T(2,128)(2,1)S(1)}, u32[]{:S(2)}, u32[]{:S(2)}) async-start(bf16[64,2,1792]{2,1,0:T(2,128)(2,1)} %bitcast.41), calls=%async_computation.7 | async-start | bytes 917504 | tf_op jit(solution)/shard_map/all_to_all | solution.py:318
  308.4 11.6 %all-to-all-done.7 = bf16[64,2,1792]{2,1,0:T(2,128)(2,1)S(1)} async-done(((bf16[64,2,1792]{2,1,0:T(2,128)(2,1)}), bf16[64,2,1792]{2,1,0:T(2,128)(2,1)S(1)}, u32[]{:S(2)}, u32[]{:S(2)}) %all-to-all-start.7) | async-done | bytes 458784 | tf_op jit(solution)/shard_map/all_to_all | solution.py:318
  321.3 15.0 %all_to_all.52 = bf16[64,2,1792]{2,1,0:T(2,128)(2,1)S(1)} all-to-all(bf16[64,2,1792]{2,1,0:T(2,128)(2,1)S(1)} %bitcast.132), channel_id=1, replica_groups=mesh['x_lo'=2,'z'=4,'y'=4,'x_hi'=2,'core'=2] {'x_lo','z','y','x_hi'}, dimensions={0} | all-to-all | bytes 917504 | tf_op jit(solution)/shard_map/all_to_all | solution.py:307
  336.9 5.1 %all_gather.55.x_ref = bf16[2,64,3584]{2,1,0:T(8,128)(2,1)S(1)} all-gather(bf16[1,64,3584]{2,1,0:T(8,128)(2,1)S(1)} %all_gather_reshape.11), channel_id=1, replica_groups=mesh['x_lo'=2,'z'=4,'y'=4,'x_hi'=2,'core'=2] {'core'}, dimensions={0}, use_global_device_ids=true | all-gather | bytes 1376256 | tf_op jit(solution)/shard_map/all_gather | solution.py:312
  342.1 3.1 copy-done.4
  345.2 3.1 copy-done.7
  348.2 4.1 expert_inner.5
  352.3 1.9 all-gather.4
  354.3 4.1 expert_down.5
  358.4 1.1 copy.94
  359.6 4.9 %all-to-all-start.9 = ((bf16[64,2,1792]{2,1,0:T(2,128)(2,1)}), bf16[64,2,1792]{2,1,0:T(2,128)(2,1)S(1)}, u32[]{:S(2)}, u32[]{:S(2)}) async-start(bf16[64,2,1792]{2,1,0:T(2,128)(2,1)} %bitcast.49), calls=%async_computation.9 | async-start | bytes 917504 | tf_op jit(solution)/shard_map/all_to_all | solution.py:318
  364.5 11.7 %all-to-all-done.9 = bf16[64,2,1792]{2,1,0:T(2,128)(2,1)S(1)} async-done(((bf16[64,2,1792]{2,1,0:T(2,128)(2,1)}), bf16[64,2,1792]{2,1,0:T(2,128)(2,1)S(1)}, u32[]{:S(2)}, u32[]{:S(2)}) %all-to-all-start.9) | async-done | bytes 458784 | tf_op jit(solution)/shard_map/all_to_all | solution.py:318
  376.7 8.3 %all-gather.6 = bf16[4,4,1792]{2,1,0:T(4,128)(2,1)S(1)} all-gather(bf16[1,4,1792]{2,1,0:T(4,128)(2,1)S(1)} %fusion.3), channel_id=7, replica_groups=mesh['x_lo'=2,'z'=4,'y'=4,'x_hi'=2,'core'=2] {'x_hi','core'}, dimensions={0}, use_global_device_ids=true | all-gather | bytes 71680 | tf_op jit(solution)/shard_map/all_gather | solution.py:324
  385.8 7.7 %copy.80 = bf16[32,128,576]{2,1,0:T(8,128)(2,1)} copy(bf16[32,128,576]{1,2,0:T(8,128)(2,1)} %collective-permute-done) | data formatting | bytes 9437184 | tf_op jit(solution)/shard_map/ppermute | solution.py:25
  393.5 2.5 copy-done.8
  396.0 2.5 copy-done.9
  398.5 17.9 %prefill.1 = bf16[512,512]{1,0:T(8,128)(2,1)} custom-call(bf16[512,576]{1,0:T(8,128)(2,1)S(1)} %bitcast.125, bf16[4096,576]{1,0:T(8,128)(2,1)S(1)} %copy-done.8, bf16[4096,576]{1,0:T(8,128)(2,1)S(1)} %bitcast.112, f32[1,4096]{1,0:T(1,128)S(1)} %bitcast.124, f32[1,4096]{1,0:T(1,128)S(1)} %bitcast.123), custom_call_target="tpu_custom_call" | custom-call | flops 9126805504 | bytes 9437184 | tf_op jit(solution)/shard_map/prefill/pallas_call | solution.py:102
  (114 shorter events, 10.7 us)
Async XLA Ops:
  7.2 1.0 copy-start
  7.2 24.8 %copy-start.18 = (s32[4]{0:T(128)S(1)}, s32[4]{0:T(128)}, u32[]{:S(2)}) copy-start(s32[4]{0:T(128)} %constant.81) | copy-start | bytes 52
  7.2 17.9 %copy-start.15 = (bf16[4,16,576]{2,1,0:T(8,128)(2,1)S(1)}, bf16[4,16,576]{2,1,0:T(8,128)(2,1)}, u32[]{:S(2)}) copy-start(bf16[4,16,576]{2,1,0:T(8,128)(2,1)} %param.16) | copy-start | bytes 221188
  7.2 24.8 %copy-start.12 = (s32[32]{0:T(128)S(1)}, s32[32]{0:T(128)}, u32[]{:S(2)}) copy-start(s32[32]{0:T(128)} %param.15) | copy-start | bytes 388
  7.2 29.3 %all-gather.12.cloned.1.call-start = ((), (), s32[]{:S(2)}) async-start(), calls=%async_computation.11 | async-start | bytes 1769472 | tf_op jit(solution)/shard_map/all_gather | solution.py:244
  8.4 16.0 %copy-start.14 = (bf16[128,576]{1,0:T(8,128)(2,1)}, bf16[128,576]{1,0:T(8,128)(2,1)S(1)}, u32[]{:S(2)}) copy-start(bf16[128,576]{1,0:T(8,128)(2,1)S(1)} %copy.97) | copy-start | bytes 442372
  8.4 10.0 %collective-permute-start.2 = (bf16[128,576]{1,0:T(8,128)(2,1)S(1)}, bf16[128,576]{1,0:T(8,128)(2,1)S(1)}, u32[]{:S(2)}, u32[]{:S(2)}) collective-permute-start(bf16[128,576]{1,0:T(8,128)(2,1)S(1)} %copy.97), channel_id=1, source_target_pairs={{0,12},{4,0},{8,4},{12,8},{1,13},{5,1},{9,5},{13,9},{2,14},{6,2},{... | collective-permute-start | bytes 442376 | tf_op jit(solution)/shard_map/ppermute | solution.py:25
  12.0 6.4 %collective-permute-start.3 = (bf16[128,576]{1,0:T(8,128)(2,1)S(1)}, bf16[128,576]{1,0:T(8,128)(2,1)S(1)}, u32[]{:S(2)}, u32[]{:S(2)}) collective-permute-start(bf16[128,576]{1,0:T(8,128)(2,1)S(1)} %copy.97), channel_id=1, source_target_pairs={{0,8},{4,12},{8,0},{12,4},{1,9},{5,13},{9,1},{13,5},{2,10},{6,14},... | collective-permute-start | bytes 442376 | tf_op jit(solution)/shard_map/ppermute | solution.py:25
  12.3 10.8 %collective-permute-start.1 = (bf16[128,576]{1,0:T(8,128)(2,1)S(1)}, bf16[128,576]{1,0:T(8,128)(2,1)S(1)}, u32[]{:S(2)}, u32[]{:S(2)}) collective-permute-start(bf16[128,576]{1,0:T(8,128)(2,1)S(1)} %copy.97), channel_id=1, source_target_pairs={{0,4},{4,8},{8,12},{12,0},{1,5},{5,9},{9,13},{13,1},{2,6},{6,10},{... | collective-permute-start | bytes 442376 | tf_op jit(solution)/shard_map/ppermute | solution.py:25
  24.3 169.6 %all-gather.10.cloned.1.call-start = ((), (), s32[]{:S(2)}) async-start(), calls=%async_computation.10 | async-start | bytes 5406720 | tf_op jit(solution)/shard_map/all_gather | solution.py:327
  26.0 15.5 %all-to-all-start = ((bf16[8,64,576]{2,1,0:T(8,128)(2,1)}), bf16[8,64,576]{2,1,0:T(8,128)(2,1)S(1)}, u32[]{:S(2)}, u32[]{:S(2)}) async-start(bf16[8,64,576]{2,1,0:T(8,128)(2,1)} %broadcast_in_dim.116), calls=%async_computation | async-start | bytes 1310720 | tf_op jit(solution)/shard_map/all_to_all | solution.py:30
  66.8 39.8 %all-to-all-start.2 = ((bf16[32,64,512]{2,1,0:T(8,128)(2,1)}), bf16[32,64,512]{2,1,0:T(8,128)(2,1)S(1)}, u32[]{:S(2)}, u32[]{:S(2)}) async-start(bf16[32,64,512]{2,1,0:T(8,128)(2,1)} %broadcast_in_dim.120), calls=%async_computation.2 | async-start | bytes 4194304 | tf_op jit(solution)/shard_map/all_to_all | solution.py:30
  73.0 6.3 %copy-start.13 = (bf16[16,512,224]{1,2,0:T(8,128)(2,1)S(1)}, bf16[16,512,224]{1,2,0:T(8,128)(2,1)}, u32[]{:S(2)}) copy-start(bf16[16,512,224]{1,2,0:T(8,128)(2,1)} %param.17) | copy-start | bytes 11010052
  77.4 164.8 %collective-permute-start.4 = (bf16[512,3584]{1,0:T(8,128)(2,1)}, bf16[512,3584]{1,0:T(8,128)(2,1)}, u32[]{:S(2)}, u32[]{:S(2)}) collective-permute-start(bf16[512,3584]{1,0:T(8,128)(2,1)} %dynamic-slice_bitcast_fusion), channel_id=1, source_target_pairs={{0,1},{1,0},{2,3},{3,2},{4,5},{5,4},{6,7},{7,6},{8,9},{9,8},{10,11... | collective-permute-start | bytes 11010056 | tf_op jit(solution)/shard_map/ppermute | solution.py:25
  79.3 2.2 copy-start.16
  113.7 21.3 %all-to-all-start.3 = ((bf16[128,4,224]{2,1,0:T(4,128)(2,1)}), bf16[128,4,224]{2,1,0:T(4,128)(2,1)S(1)}, u32[]{:S(2)}, u32[]{:S(2)}) async-start(bf16[128,4,224]{2,1,0:T(4,128)(2,1)} %bitcast.15), calls=%async_computation.3 | async-start | bytes 524288 | tf_op jit(solution)/shard_map/all_to_all | solution.py:277
  137.3 84.6 %all-to-all-start.4 = ((bf16[64,2,1792]{2,1,0:T(2,128)(2,1)}), bf16[64,2,1792]{2,1,0:T(2,128)(2,1)S(1)}, u32[]{:S(2)}, u32[]{:S(2)}) async-start(bf16[64,2,1792]{2,1,0:T(2,128)(2,1)} %bitcast.23), calls=%async_computation.4 | async-start | bytes 917504 | tf_op jit(solution)/shard_map/all_to_all | solution.py:307
  193.9 27.7 %copy-start.17 = (f32[3,4,8]{2,1,0:T(4,128)S(1)}, f32[3,4,8]{2,1,0:T(4,128)}, u32[]{:S(2)}) copy-start(f32[3,4,8]{2,1,0:T(4,128)} %param.24) | copy-start | bytes 1156
  193.9 35.6 %copy-start.10 = (f32[7168]{0:T(1024)S(1)}, f32[7168]{0:T(1024)}, u32[]{:S(2)}) copy-start(f32[7168]{0:T(1024)} %param.19) | copy-start | bytes 86020
  201.5 184.3 %collective-permute-start = (bf16[32,128,576]{1,2,0:T(8,128)(2,1)}, bf16[32,128,576]{1,2,0:T(8,128)(2,1)}, u32[]{:S(2)}, u32[]{:S(2)}) collective-permute-start(bf16[32,128,576]{1,2,0:T(8,128)(2,1)} %copy.79), channel_id=1, source_target_pairs={{0,1},{1,0},{2,3},{3,2},{4,5},{5,4},{6,7},{7,6},{8,9},{9,8},{10,11... | collective-permute-start | bytes 14155784 | tf_op jit(solution)/shard_map/ppermute | solution.py:25
  229.5 12.6 %slice-start = ((s8[7340032]{0:T(1024)(128)(4,1)}), s8[4194304]{0:T(1024)(128)(4,1)S(1)}, s32[]{:S(2)}) async-start(s8[7340032]{0:T(1024)(128)(4,1)} %bitcast.96), calls=%async_computation.12 | async-start | bytes 8388608
  229.5 3.2 copy-start.2
  232.8 3.2 copy-start.5
  236.0 6.2 %slice-start.1 = ((s8[7340032]{0:T(1024)(128)(4,1)}), s8[3145728]{0:T(1024)(128)(4,1)S(1)}, s32[]{:S(2)}) async-start(s8[7340032]{0:T(1024)(128)(4,1)} %bitcast.96), calls=%async_computation.13 | async-start | bytes 6291456
  247.5 16.5 %all-to-all-start.5 = ((bf16[64,2,1792]{2,1,0:T(2,128)(2,1)}), bf16[64,2,1792]{2,1,0:T(2,128)(2,1)S(1)}, u32[]{:S(2)}, u32[]{:S(2)}) async-start(bf16[64,2,1792]{2,1,0:T(2,128)(2,1)} %bitcast.33), calls=%async_computation.5 | async-start | bytes 917504 | tf_op jit(solution)/shard_map/all_to_all | solution.py:318
  280.9 17.5 %slice-start.2 = ((s8[7340032]{0:T(1024)(128)(4,1)}), s8[4194304]{0:T(1024)(128)(4,1)S(1)}, s32[]{:S(2)}) async-start(s8[7340032]{0:T(1024)(128)(4,1)} %bitcast.99), calls=%async_computation.14 | async-start | bytes 8388608
  286.2 3.1 copy-start.3
  289.3 3.1 copy-start.6
  292.3 6.0 %slice-start.3 = ((s8[7340032]{0:T(1024)(128)(4,1)}), s8[3145728]{0:T(1024)(128)(4,1)S(1)}, s32[]{:S(2)}) async-start(s8[7340032]{0:T(1024)(128)(4,1)} %bitcast.99), calls=%async_computation.15 | async-start | bytes 6291456
  303.7 16.4 %all-to-all-start.7 = ((bf16[64,2,1792]{2,1,0:T(2,128)(2,1)}), bf16[64,2,1792]{2,1,0:T(2,128)(2,1)S(1)}, u32[]{:S(2)}, u32[]{:S(2)}) async-start(bf16[64,2,1792]{2,1,0:T(2,128)(2,1)} %bitcast.41), calls=%async_computation.7 | async-start | bytes 917504 | tf_op jit(solution)/shard_map/all_to_all | solution.py:318
  336.9 17.3 %slice-start.4 = ((s8[7340032]{0:T(1024)(128)(4,1)}), s8[4194304]{0:T(1024)(128)(4,1)S(1)}, s32[]{:S(2)}) async-start(s8[7340032]{0:T(1024)(128)(4,1)} %bitcast.102), calls=%async_computation.16 | async-start | bytes 8388608
  342.1 3.1 copy-start.4
  345.2 3.1 copy-start.7
  348.2 6.0 %slice-start.5 = ((s8[7340032]{0:T(1024)(128)(4,1)}), s8[3145728]{0:T(1024)(128)(4,1)S(1)}, s32[]{:S(2)}) async-start(s8[7340032]{0:T(1024)(128)(4,1)} %bitcast.102), calls=%async_computation.17 | async-start | bytes 6291456
  359.6 16.6 %all-to-all-start.9 = ((bf16[64,2,1792]{2,1,0:T(2,128)(2,1)}), bf16[64,2,1792]{2,1,0:T(2,128)(2,1)S(1)}, u32[]{:S(2)}, u32[]{:S(2)}) async-start(bf16[64,2,1792]{2,1,0:T(2,128)(2,1)} %bitcast.49), calls=%async_computation.9 | async-start | bytes 917504 | tf_op jit(solution)/shard_map/all_to_all | solution.py:318
  385.8 7.7 %copy-start.11 = (bf16[16,32,576]{2,1,0:T(8,128)(2,1)S(1)}, bf16[16,32,576]{2,1,0:T(8,128)(2,1)}, u32[]{:S(2)}) copy-start(bf16[16,32,576]{2,1,0:T(8,128)(2,1)} %param.13) | copy-start | bytes 1769476
  393.5 2.5 copy-start.8
  396.0 2.5 copy-start.9
  398.4 17.9 %copy-start.1 = (bf16[256,576]{0,1:T(8,128)(2,1)S(1)}, bf16[256,576]{0,1:T(8,128)(2,1)}, u32[]{:S(2)}) copy-start(bf16[256,576]{0,1:T(8,128)(2,1)} %param.14) | copy-start | bytes 884740
Sparse Core Ops, SparseCore 0:
  24.5 11.9 all-gather.11
  38.1 155.7 all-gather.9

commit v2 on v1

v2 whole, which is shorter than its diff:
```python
import functools

import jax
import jax.numpy as jnp
from jax import lax
from jax.experimental import pallas as pl
from jax.experimental.pallas import tpu as pltpu
from jax.sharding import Mesh, PartitionSpec as P

KV_RANK = 512
STEPS = 3
SLOTS = 2
SCALE = 0.07216878364870322
MASKED = -1e30

SPLIT = {"ctx": (("x_lo", 2), ("z", 4), ("y", 4)), "head": (("x_hi", 2), ("core", 2))}
CTX = ("x_lo", "z", "y")
HEAD = ("x_hi", "core")
SHARDS = ("x_lo", "z")
LANE = CTX + ("x_hi",)


def shift(x, axis, by):
    n = lax.axis_size(axis)
    return lax.ppermute(x, axis, [(i, (i + by) % n) for i in range(n)])


def spread(x, axes):
    n = lax.axis_size(axes)
    return lax.all_to_all(jnp.broadcast_to(x[None], (n,) + x.shape), axes, 0, 0, tiled=True)


def dot_t(a, b):
    return lax.dot_general(a, b, (((1,), (1,)), ((), ())), preferred_element_type=jnp.float32)


def tie(x, after):
    anywhere = pl.BlockSpec(memory_space=pl.ANY)
    return pl.pallas_call(
        lambda x_ref, after_ref, out_ref: None,
        in_specs=[anywhere, anywhere],
        out_specs=anywhere,
        out_shape=jax.ShapeDtypeStruct(x.shape, x.dtype),
        input_output_aliases={0: 0},
        compiler_params=pltpu.CompilerParams(vmem_limit_bytes=56 << 20),
        cost_estimate=pl.CostEstimate(flops=0, bytes_accessed=0, transcendentals=0),
        name="tie",
    )(x, after)


def take(ref, at):
    return [ref[i] for i in at]


def dec_attn_kernel(q_ref, own_ref, other_ref, bias_ref, out_ref):
    n = own_ref.shape[0]
    keys = jnp.concatenate(take(own_ref, range(n)) + take(other_ref, range(n)), axis=1)
    s = jnp.dot(q_ref[...], keys, preferred_element_type=jnp.float32) * SCALE + bias_ref[...]
    top = jnp.max(s, axis=1, keepdims=True)
    p = jnp.exp(s - top)
    total = jnp.sum(p, axis=1, keepdims=True)
    acc = dot_t(p.astype(jnp.bfloat16), keys[:KV_RANK])
    out_ref[:, :KV_RANK] = (acc / total).astype(jnp.bfloat16)
    lse = jnp.broadcast_to(top + jnp.log(total), (q_ref.shape[0], 128))
    hi = lse.astype(jnp.bfloat16).astype(jnp.float32)
    mid = (lse - hi).astype(jnp.bfloat16).astype(jnp.float32)
    low = lse - hi - mid
    lane = lax.broadcasted_iota(jnp.int32, lse.shape, 1)
    out_ref[:, KV_RANK:] = jnp.where(
        lane == 0, hi, jnp.where(lane == 1, mid, jnp.where(lane == 2, low, 0.0))
    ).astype(jnp.bfloat16)


def decode_attention(q, own, other, bias):
    rows, width = q.shape
    return pl.pallas_call(
        dec_attn_kernel,
        out_shape=jax.ShapeDtypeStruct((rows, KV_RANK + 128), jnp.bfloat16),
        compiler_params=pltpu.CompilerParams(vmem_limit_bytes=16 << 20),
        cost_estimate=pl.CostEstimate(
            flops=2 * rows * bias.shape[1] * (width + KV_RANK),
            bytes_accessed=4 * rows * width,
            transcendentals=rows * bias.shape[1],
        ),
        name="decode_attention",
    )(q, own, other, bias)


def combine_kernel(parts_ref, out_ref):
    n, rows, _ = parts_ref.shape
    lses = [
        jnp.sum(parts_ref[i, :, KV_RANK:].astype(jnp.float32), axis=1, keepdims=True)
        for i in range(n)
    ]
    top = functools.reduce(jnp.maximum, lses)
    shares = [jnp.exp(x - top) for x in lses]
    total = functools.reduce(jnp.add, shares)
    acc = sum(shares[i] * parts_ref[i, :, :KV_RANK].astype(jnp.float32) for i in range(n))
    out_ref[...] = (acc / total).astype(jnp.bfloat16)


def project_kernel(sides_ref, lat_ref, own_ref, other_ref, keep_ref, send_ref):
    heads, _, rank = own_ref.shape
    own = other = None
    for h in range(heads):
        lat = lat_ref[:, h * rank : (h + 1) * rank]
        mine, theirs = dot_t(lat, own_ref[h]), dot_t(lat, other_ref[h])
        own = mine if own is None else own + mine
        other = theirs if other is None else other + theirs
    same = sides_ref[0] == sides_ref[1]
    keep_ref[...] = jnp.where(same, own, other)
    send_ref[...] = jnp.where(same, other, own).astype(jnp.bfloat16)


def project(sides, latent, w_own, w_other):
    rows, depth = latent.shape
    heads, cols, rank = w_other.shape
    whole = pl.BlockSpec((rows, cols), lambda i, sides: (0, 0))
    return pl.pallas_call(
        project_kernel,
        grid_spec=pltpu.PrefetchScalarGridSpec(
            num_scalar_prefetch=1,
            grid=(1,),
            in_specs=[
                pl.BlockSpec((rows, depth), lambda i, sides: (0, 0)),
                pl.BlockSpec((heads, cols, rank), lambda i, sides: (sides[0], 0, 0)),
                pl.BlockSpec((heads, cols, rank), lambda i, sides: (0, 0, 0)),
            ],
            out_specs=[whole, whole],
        ),
        out_shape=[
            jax.ShapeDtypeStruct((rows, cols), jnp.float32),
            jax.ShapeDtypeStruct((rows, cols), jnp.bfloat16),
        ],
        compiler_params=pltpu.CompilerParams(vmem_limit_bytes=20 << 20),
        cost_estimate=pl.CostEstimate(
            flops=4 * rows * depth * cols, bytes_accessed=4 * depth * cols, transcendentals=0
        ),
        name="project",
    )(sides, latent, w_own, w_other)


def prefill_kernel(q_ref, own_ref, other_ref, bias_ref, *rest):
    out_ref, done_ref, top_ref, total_ref, acc_ref = rest[-5:]
    step = pl.program_id(0)

    @pl.when(step == 0)
    def _():
        top_ref[...] = jnp.full_like(top_ref, MASKED)
        total_ref[...] = jnp.zeros_like(total_ref)
        acc_ref[...] = jnp.zeros_like(acc_ref)
        done_ref[...] = jnp.zeros_like(done_ref)

    n = own_ref.shape[0]
    keys = jnp.concatenate(take(own_ref, range(n)) + take(other_ref, range(n)), axis=1)
    s = jnp.dot(q_ref[...], keys, preferred_element_type=jnp.float32) * SCALE + bias_ref[0]
    old = top_ref[...]
    top = jnp.maximum(old, jnp.max(s, axis=1, keepdims=True))
    p = jnp.exp(s - top)
    fade = jnp.exp(old - top)
    total_ref[...] = total_ref[...] * fade + jnp.sum(p, axis=1, keepdims=True)
    acc_ref[...] = acc_ref[...] * fade + dot_t(p.astype(jnp.bfloat16), keys[:KV_RANK])
    top_ref[...] = top

    @pl.when(step == pl.num_programs(0) - 1)
    def _():
        out_ref[...] = (acc_ref[...] / total_ref[...]).astype(jnp.bfloat16)


def prefill(piece, pieces, q, own, other, bias, after, so_far):
    rows, width = q.shape
    part = rows // pieces
    count = own.shape[0]
    group = 4
    positions = 2 * group * own.shape[2]
    kv_spec = pl.BlockSpec((group,) + own.shape[1:], lambda i: (i, 0, 0))
    anywhere = pl.BlockSpec(memory_space=pl.ANY)
    extra = [after] + ([] if so_far is None else [so_far])
    return pl.pallas_call(
        prefill_kernel,
        grid=(count // group,),
        in_specs=[
            pl.BlockSpec((part, width), lambda i: (piece, 0)),
            kv_spec,
            kv_spec,
            pl.BlockSpec((1, 1, positions), lambda i: (i, 0, 0)),
        ]
        + [anywhere] * len(extra),
        out_specs=[
            pl.BlockSpec((part, KV_RANK), lambda i: (piece, 0)),
            pl.BlockSpec((8, 128), lambda i: (0, 0)),
        ],
        out_shape=[
            jax.ShapeDtypeStruct((rows, KV_RANK), jnp.bfloat16),
            jax.ShapeDtypeStruct((8, 128), jnp.float32),
        ],
        input_output_aliases={} if so_far is None else {5: 0},
        scratch_shapes=[
            pltpu.VMEM((part, 1), jnp.float32),
            pltpu.VMEM((part, 1), jnp.float32),
            pltpu.VMEM((part, KV_RANK), jnp.float32),
        ],
        compiler_params=pltpu.CompilerParams(vmem_limit_bytes=56 << 20),
        cost_estimate=pl.CostEstimate(
            flops=4 * part * count * own.shape[2] * (width + KV_RANK),
            bytes_accessed=4 * count * own.shape[2] * width,
            transcendentals=2 * part * count * own.shape[2],
        ),
        name="prefill",
    )(q, own, other, bias, *extra)


def inner_kernel(x_ref, gain_ref, gate_ref, up_ref, out_ref, x_scr, gate_acc, up_acc):
    cores, pieces, slots, quarter = x_ref.shape
    steps, _, chunk = x_scr.shape
    step = pl.program_id(0)

    @pl.when(step == 0)
    def _():
        square = 0.0
        for core in range(cores):
            for x_hi in range(2):
                x = jnp.concatenate(
                    [x_ref[core, piece].astype(jnp.float32) for piece in range(x_hi, pieces, 2)], axis=0
                )
                square = square + jnp.sum(x * x, axis=1, keepdims=True)
                for part in range(quarter // chunk):
                    x_scr[(core * 2 + x_hi) * (quarter // chunk) + part] = x[:, part * chunk : (part + 1) * chunk].astype(jnp.bfloat16)
        scale = lax.rsqrt(square / (steps * chunk) + 1e-06)
        for part in range(steps):
            x = x_scr[part].astype(jnp.float32) * scale * gain_ref[:, part * chunk : (part + 1) * chunk]
            x_scr[part] = x.astype(jnp.bfloat16)
        gate_acc[...] = jnp.zeros_like(gate_acc)
        up_acc[...] = jnp.zeros_like(up_acc)

    x = x_scr[step]
    gate_acc[...] += jnp.dot(x, gate_ref[...], preferred_element_type=jnp.float32)
    up_acc[...] += jnp.dot(x, up_ref[...], preferred_element_type=jnp.float32)

    @pl.when(step == pl.num_programs(0) - 1)
    def _():
        out_ref[...] = (jax.nn.silu(gate_acc[...]) * up_acc[...]).astype(jnp.bfloat16)


def expert_inner(x, gain, w_gate, w_up):
    rows, (depth, hidden) = x.shape[1] // 2 * x.shape[2], w_gate.shape
    chunk = 896
    w_spec = pl.BlockSpec((chunk, hidden), lambda i: (i, 0))
    return pl.pallas_call(
        inner_kernel,
        grid=(depth // chunk,),
        in_specs=[
            pl.BlockSpec(x.shape, lambda i: (0, 0, 0, 0)),
            pl.BlockSpec((1, depth), lambda i: (0, 0)),
            w_spec,
            w_spec,
        ],
        out_specs=pl.BlockSpec((rows, hidden), lambda i: (0, 0)),
        out_shape=jax.ShapeDtypeStruct((rows, hidden), jnp.bfloat16),
        scratch_shapes=[
            pltpu.VMEM((depth // chunk, rows, chunk), jnp.bfloat16),
            pltpu.VMEM((rows, hidden), jnp.float32),
            pltpu.VMEM((rows, hidden), jnp.float32),
        ],
        compiler_params=pltpu.CompilerParams(vmem_limit_bytes=56 << 20),
        cost_estimate=pl.CostEstimate(
            flops=4 * rows * depth * hidden, bytes_accessed=4 * depth * hidden, transcendentals=rows * hidden
        ),
        name="expert_inner",
    )(x, gain, w_gate, w_up)


def down_kernel(core_ref, inner_ref, own_ref, other_ref, out_ref):
    core = core_ref[0]
    out_ref[...] = (
        jnp.dot(inner_ref[core], own_ref[...], preferred_element_type=jnp.float32)
        + jnp.dot(inner_ref[1 - core], other_ref[...], preferred_element_type=jnp.float32)
    ).astype(jnp.bfloat16)


def expert_down(core, inner, w_down, w_other):
    _, rows, hidden = inner.shape
    width = w_other.shape[1]
    block = 896
    steps = width // block
    return pl.pallas_call(
        down_kernel,
        grid_spec=pltpu.PrefetchScalarGridSpec(
            num_scalar_prefetch=1,
            grid=(steps,),
            in_specs=[
                pl.BlockSpec(inner.shape, lambda i, core: (0, 0, 0)),
                pl.BlockSpec((hidden, block), lambda i, core: (0, core[0] * steps + i)),
                pl.BlockSpec((hidden, block), lambda i, core: (0, i)),
            ],
            out_specs=pl.BlockSpec((rows, block), lambda i, core: (0, i)),
        ),
        out_shape=jax.ShapeDtypeStruct((rows, width), jnp.bfloat16),
        compiler_params=pltpu.CompilerParams(vmem_limit_bytes=56 << 20),
        cost_estimate=pl.CostEstimate(
            flops=4 * rows * hidden * width, bytes_accessed=4 * hidden * width, transcendentals=0
        ),
        name="expert_down",
    )(core, inner, w_down, w_other)


def collect_kernel(weight_ref, returned_ref, state_ref, *rest):
    out_ref = rest[-1]
    added = jnp.dot(
        weight_ref[...],
        returned_ref[...].astype(jnp.float32),
        precision=lax.Precision.HIGHEST,
        preferred_element_type=jnp.float32,
    )
    out_ref[...] = (state_ref[...].astype(jnp.float32) + added).astype(jnp.bfloat16)


def collect_rows(weight, returned, state, extra):
    vmem = pl.BlockSpec(memory_space=pltpu.VMEM)
    return pl.pallas_call(
        collect_kernel,
        in_specs=[vmem] * 3 + [pl.BlockSpec(memory_space=pl.ANY)] * len(extra),
        out_specs=vmem,
        out_shape=jax.ShapeDtypeStruct(state.shape, state.dtype),
        compiler_params=pltpu.CompilerParams(vmem_limit_bytes=8 << 20),
        name="collect_rows",
    )(weight, returned, state, *extra)


def per_device(
    stretch_queries,
    cache_latent,
    doc_lengths,
    decode_queries,
    w_attn_out,
    decode_hidden,
    norm_gain,
    w_gate,
    w_up,
    w_down,
    routes,
    gate_weights,
):
    tokens, heads, width = stretch_queries.shape
    rows, dec_heads, _ = decode_queries.shape
    block = cache_latent.shape[0]
    half = block // 2
    ctx_size = lax.axis_size(CTX)
    model = decode_hidden.shape[1]
    core = lax.axis_index("core")
    x_hi = lax.axis_index("x_hi")
    x_lo = lax.axis_index("x_lo")
    quarter = model // 4
    my_quarter = core * 2 + x_hi

    w_out = jnp.swapaxes(w_attn_out, 1, 2)
    w_out_other = shift(
        lax.dynamic_slice_in_dim(w_out, (1 - x_lo) * (dec_heads // 2), dec_heads // 2, 0), "x_lo", 1
    )

    mine = lax.dynamic_slice_in_dim(cache_latent.T, core * half, half, 1)

    line = jnp.stack([mine] + [shift(mine, "y", by) for by in (1, 3, 2)])
    dec_q = decode_queries.reshape(rows * dec_heads, width)
    group_q = spread(dec_q, SHARDS)
    shards = group_q.shape[0]
    line_other = shift(line, "core", 1)
    y = lax.axis_index("y")
    line_at = lax.axis_index(SHARDS) * 4 + (y - jnp.array([0, 1, 3, 2], jnp.int32)) % 4
    line_len = jnp.sum(
        jnp.where(line_at[:, None] == jnp.arange(doc_lengths.shape[0])[None, :], doc_lengths[None, :], 0), axis=1
    )
    place = jnp.arange(half, dtype=jnp.int32)

    def bias_of(which, lengths):
        usable = place + which * half < lengths[..., None]
        return jnp.where(usable, 0.0, MASKED).astype(jnp.float32)

    line_bias = jnp.stack([bias_of(core, line_len), bias_of(1 - core, line_len)])
    parts = decode_attention(
        group_q.reshape(shards * rows * dec_heads, width), line, line_other, line_bias.reshape(1, 4 * block)
    )
    parts = lax.all_to_all(
        parts.reshape(shards, rows * dec_heads, KV_RANK + 128), SHARDS, 0, 0, tiled=True
    )
    dec_latent = pl.pallas_call(
        combine_kernel,
        out_shape=jax.ShapeDtypeStruct((rows * dec_heads, KV_RANK), jnp.bfloat16),
        compiler_params=pltpu.CompilerParams(vmem_limit_bytes=8 << 20),
        name="combine_shards",
    )(parts)

    depth = dec_heads // 2 * KV_RANK
    latent_halves = jnp.swapaxes(dec_latent.reshape(rows, 2, depth), 0, 1)
    latent_halves = jnp.broadcast_to(latent_halves[:, None], (2, ctx_size // 2, rows, depth))
    all_latent = lax.all_to_all(
        latent_halves.reshape(ctx_size, rows, depth), CTX, 0, 0, tiled=True
    )
    cols = w_out.shape[1]
    sides = jnp.stack([x_lo, core]).astype(jnp.int32)
    keep, send = project(sides, all_latent.reshape(ctx_size * rows, depth), w_out, w_out_other)
    attn_cols = (keep + shift(send, "core", 1).astype(jnp.float32)).astype(jnp.bfloat16)
    attn_cols = jnp.broadcast_to(
        attn_cols.reshape(ctx_size, 1, rows, cols), (ctx_size, 2, rows, cols)
    ).reshape(ctx_size * 2, rows, cols)
    attn_parts = lax.all_to_all(attn_cols, LANE, 0, 0, tiled=True)
    attn_parts = attn_parts.reshape(2, 2, 2, 4, 2, rows, cols)
    attn_parts = lax.dynamic_index_in_dim(attn_parts, x_hi, 1, keepdims=False)
    attn_out = jnp.sum(attn_parts.astype(jnp.float32), axis=(0, 3)).astype(jnp.bfloat16)
    attn_out = jnp.swapaxes(attn_out.reshape(8, rows, cols), 0, 1).reshape(rows, quarter)
    hidden_quarter = lax.dynamic_slice_in_dim(decode_hidden, my_quarter * quarter, quarter, 1)
    state = (hidden_quarter.astype(jnp.float32) + attn_out.astype(jnp.float32)).astype(jnp.bfloat16)

    experts = jnp.arange(ctx_size, dtype=jnp.int32)
    hits = routes[..., None] == experts
    used = jnp.any(hits, axis=2)
    weight = jnp.sum(jnp.where(hits, gate_weights[..., None], 0.0), axis=2)
    counted = used.astype(jnp.int32)
    earlier = jnp.cumsum(counted, axis=1) - counted
    placed = used[..., None] & (earlier[..., None] == jnp.arange(SLOTS, dtype=jnp.int32))
    dispatch = jnp.moveaxis(placed, 1, -1).astype(jnp.bfloat16)
    dispatch = dispatch.reshape(STEPS, ctx_size * SLOTS, rows)
    collect = jnp.where(placed, weight[..., None], 0.0)
    collect = jnp.broadcast_to(collect[:, :, :, None, :], (STEPS, rows, ctx_size, 2, SLOTS))
    collect = collect.reshape(STEPS, rows, ctx_size * 2 * SLOTS)

    other_cols = lax.dynamic_slice_in_dim(w_down[0], (1 - core) * (model // 2), model // 2, 1)
    w_other = shift(other_cols, "core", 1)
    core_arr = core.astype(jnp.int32).reshape(1)
    gain = norm_gain.reshape(1, model)

    line_late = tie(line, dec_latent)
    gathered = lax.all_gather(line_late, SHARDS, axis=0).reshape(ctx_size, width, half)
    gathered_at = (
        jnp.arange(shards, dtype=jnp.int32)[:, None] * 4 + (y - jnp.array([0, 1, 3, 2], jnp.int32)) % 4
    ).reshape(ctx_size)
    gathered_len = jnp.sum(
        jnp.where(gathered_at[:, None] == jnp.arange(ctx_size)[None, :], doc_lengths[None, :], 0), axis=1
    )
    bias = jnp.stack(
        [bias_of(core, gathered_len).reshape(-1, 4, half), bias_of(1 - core, gathered_len).reshape(-1, 4, half)],
        axis=1,
    ).reshape(ctx_size // 4, 1, 8 * half)
    flat_q = stretch_queries.reshape(tokens * heads, width)
    stretch_latent = None

    for step in range(STEPS):
        last = step == STEPS - 1
        outgoing = jnp.dot(dispatch[step], state, preferred_element_type=jnp.float32)
        outgoing = outgoing.astype(jnp.bfloat16).reshape(ctx_size, 1, SLOTS, quarter)
        outgoing = jnp.broadcast_to(outgoing, (ctx_size, 2, SLOTS, quarter))
        outgoing = outgoing.reshape(ctx_size * 2, SLOTS, quarter)
        received = lax.all_to_all(outgoing, LANE, 0, 0, tiled=True)
        if last:
            stretch_latent, token = prefill(0, 2, flat_q, gathered, others, bias, state, None)
            received = tie(received, token)
        received = lax.all_gather(received, "core", axis=0)
        inner = expert_inner(received, gain, w_gate[0], w_up[0])
        inner = lax.all_gather(inner, "core", axis=0)
        partial_out = expert_down(core_arr, inner, w_down[0], w_other)
        if step == STEPS - 2:
            gathered = tie(gathered, partial_out)
            others = shift(gathered, "core", 1)
        extra = []
        if last:
            stretch_latent, token = prefill(1, 2, flat_q, gathered, others, bias, partial_out, stretch_latent)
            extra = [token]
        partial_out = partial_out.reshape(ctx_size, SLOTS, 2, quarter)
        partial_out = jnp.swapaxes(partial_out, 1, 2).reshape(ctx_size * 2, SLOTS, quarter)
        returned = lax.all_to_all(partial_out, LANE, 0, 0, tiled=True)
        returned = returned.reshape(ctx_size * 2 * SLOTS, quarter)
        state = collect_rows(collect[step], returned, state, extra)
    decode_out = lax.all_gather(state, HEAD, axis=0)
    decode_out = decode_out.reshape(2, 2, rows, quarter).transpose(2, 1, 0, 3).reshape(rows, model)
    return stretch_latent.reshape(tokens, heads, KV_RANK), decode_out


def solution(mesh):
    names = [name for axis in mesh.axis_names for name, _ in SPLIT[axis]]
    sizes = [size for axis in mesh.axis_names for _, size in SPLIT[axis]]
    fine = Mesh(mesh.devices.reshape(sizes), names)
    return jax.shard_map(
        per_device,
        mesh=fine,
        in_specs=(
            P(CTX, HEAD, None),
            P(CTX, None),
            P(),
            P(CTX, HEAD, None),
            P(HEAD, None, CTX),
            P(CTX, None),
            P(),
            P(CTX, None, HEAD),
            P(CTX, None, HEAD),
            P(CTX, HEAD, None),
            P(None, CTX, None),
            P(None, CTX, None),
        ),
        out_specs=(P(CTX, HEAD, None), P(CTX, None)),
        check_vma=False,
    )
```

time: 425 us -> 388 us (0.913)
  local copies, waits for them, and re-layouts: 66.1 us -> 28.8 us
  Pallas kernels: 46.3 us -> 77.1 us
  waiting for transfers between devices: 142 us -> 127 us
  blocking collectives: 80.6 us -> 68 us
  matrix products: 5.64 us -> 0.81 us
    all_to_all x2 -> x4, waiting for transfers between devices: 11.9 us -> 98.5 us  [the longest x1 79.8 us: per_device(): lax.all_to_all(latent_halves.reshape(ctx_size, rows, depth), CTX, 0, 0, t...]
    all_gather x2 -> x1, waiting for transfers between devices: 55.7 us -> 0.01 us  [per_device(): lax.all_gather(line_late, SHARDS, axis=0).reshape(ctx_size, width, half)]
    all_to_all x2 -> x1, waiting for transfers between devices: 28.4 us -> 5.07 us  [spread(): lax.all_to_all(jnp.broadcast_to(x[None], (n,) + x.shape), axes, 0, 0, til...]
    unnamed x51 -> x24, local copies, waits for them, and re-layouts: 24.9 us -> 4.91 us
    pallas_call x3, Pallas kernels: 12.2 us -> 31.6 us  [expert_inner(): pl.pallas_call(inner_kernel, grid=(depth // chunk,), in_specs=[pl.BlockSp...]
    all_to_all x2 -> x1, blocking collectives: 30 us -> 15 us  [per_device(): received = lax.all_to_all(outgoing, LANE, 0, 0, tiled=True)]
    all_to_all x3, waiting for transfers between devices: 34.7 us -> 22.9 us  [per_device(): returned = lax.all_to_all(partial_out, LANE, 0, 0, tiled=True)]
    pallas_call x2 -> x10, Pallas kernels: 19.8 us -> 29.6 us  [the longest x2 24.4 us: prefill(): pl.pallas_call(prefill_kernel, grid=(count // group,), in_specs=[pl.Block...]
  transfers between devices with their start and end apart: 14 -> 17, of which waited for: 10 -> 7; matrix products, arithmetic and copies ran while one was open for 9% -> 6% of each run, Pallas kernels for 7% -> 15%
where the time goes in v2:
time: 388 us; the launch traced here: 385 us
  waiting for transfers between devices  127 us (33%)
  Pallas kernels  77.1 us (20%)
  blocking collectives  68 us (18%)
  starting transfers between devices  65.4 us (17%)
  local copies, waits for them, and re-layouts  28.8 us (7%)
  between operations  14.5 us (4%)
    all_to_all x1, waiting for transfers between devices, per_device(): lax.all_to_all(latent_halves.reshape(ctx_size, rows, depth), CTX, 0, 0, t...  79.8 us
    pallas_call x3, Pallas kernels, expert_inner(): pl.pallas_call(inner_kernel, grid=(depth // chunk,), in_specs=[pl.BlockSp...  31.6 us
    pallas_call x2, Pallas kernels, prefill(): pl.pallas_call(prefill_kernel, grid=(count // group,), in_specs=[pl.Block...  24.4 us
    all_to_all x3, waiting for transfers between devices, per_device(): returned = lax.all_to_all(partial_out, LANE, 0, 0, tiled=True)  22.9 us
    all_to_all x3, starting transfers between devices, per_device(): returned = lax.all_to_all(partial_out, LANE, 0, 0, tiled=True)  19.2 us
    all_gather x3, blocking collectives, per_device(): received = lax.all_gather(received, 'core', axis=0)  18.9 us
    ppermute x8, starting transfers between devices, shift(): return lax.ppermute(x, axis, [(i, (i + by) % n) for i in range(n)])  17.4 us
    pallas_call x3, Pallas kernels, expert_down(): pl.pallas_call(down_kernel, grid_spec=pltpu.PrefetchScalarGridSpec(num_sc...  15.7 us
  transfers between devices with their start and end apart: 17, of which 7 were waited for; matrix products, arithmetic and copies ran while one was open for 6% of the time, Pallas kernels for 15%

profile of v2, /device:TPU:1, one launch (start us, length us, event | category | flops | bytes accessed | tf_op | source)
XLA Modules:
  0.0 385.3 jit_solution(7925545909281728152)
XLA Ops:
  7.2 1.0 dynamic-slice_bitcast_fusion.2
  8.1 3.6 collective-permute-start.1
  11.8 1.6 collective-permute-start.2
  13.4 1.8 broadcast_in_dim.148
  15.2 6.0 %all-to-all-start = ((bf16[8,64,576]{2,1,0:T(8,128)(2,1)}), bf16[8,64,576]{2,1,0:T(8,128)(2,1)S(1)}, u32[]{:S(2)}, u32[]{:S(2)}) async-start(bf16[8,64,576]{2,1,0:T(8,128)(2,1)} %broadcast_in_dim.148), calls=%async_computation | async-start | bytes 1310720 | tf_op jit(solution)/shard_map/all_to_all | solution.py:30
  21.2 0.7 broadcast_add_fusion.1
  22.0 1.9 collective-permute-start.3
  24.2 5.1 %all-to-all-done = bf16[8,64,576]{2,1,0:T(8,128)(2,1)S(1)} async-done(((bf16[8,64,576]{2,1,0:T(8,128)(2,1)}), bf16[8,64,576]{2,1,0:T(8,128)(2,1)S(1)}, u32[]{:S(2)}, u32[]{:S(2)}) %all-to-all-start) | async-done | bytes 589856 | tf_op jit(solution)/shard_map/all_to_all | solution.py:30
  29.2 1.9 decode_attention.1
  31.1 15.6 %all_to_all.50.parts_ref = bf16[8,64,640]{2,1,0:T(8,128)(2,1)S(1)} all-to-all(bf16[8,64,640]{2,1,0:T(8,128)(2,1)S(1)} %bitcast.88), channel_id=1, replica_groups=mesh['x_lo'=2,'z'=4,'y'=4,'x_hi'=2,'core'=2] {'x_lo','z'}, dimensions={0} | all-to-all | bytes 1310720 | tf_op jit(solution)/shard_map/all_to_all | solution.py:383
  47.0 0.6 copy-done.2
  47.7 2.8 dynamic-slice_bitcast_fusion.1
  50.5 4.1 %dynamic-slice_bitcast_fusion = bf16[512,3584]{1,0:T(8,128)(2,1)} fusion(bf16[1,512,7168]{2,1,0:T(8,128)(2,1)} %param.23, s32[]{:T(128)S(6)} %select_n.102), kind=kLoop, calls=%fused_computation | loop fusion | bytes 7340036 | tf_op jit(solution)/shard_map/dynamic_slice | solution.py:427
  54.6 3.2 collective-permute-start.6
  57.9 1.5 broadcast_in_dim.159
  59.3 4.8 %all-to-all-start.2 = ((bf16[32,4,4096]{2,1,0:T(4,128)(2,1)}), bf16[32,4,4096]{2,1,0:T(4,128)(2,1)}, u32[]{:S(2)}, u32[]{:S(2)}) async-start(bf16[32,4,4096]{2,1,0:T(4,128)(2,1)} %bitcast.17), calls=%async_computation.2 | async-start | bytes 2097152 | tf_op jit(solution)/shard_map/all_to_all | solution.py:396
  64.4 79.8 %all-to-all-done.2 = bf16[32,4,4096]{2,1,0:T(4,128)(2,1)} async-done(((bf16[32,4,4096]{2,1,0:T(4,128)(2,1)}), bf16[32,4,4096]{2,1,0:T(4,128)(2,1)}, u32[]{:S(2)}, u32[]{:S(2)}) %all-to-all-start.2) | async-done | bytes 1048608 | tf_op jit(solution)/shard_map/all_to_all | solution.py:396
  144.3 1.3 reshape.321.lat_ref
  145.6 2.0 copy-done
  147.7 1.9 project.1
  149.6 6.9 %collective-permute-start.5 = (bf16[128,224]{1,0:T(8,128)(2,1)S(1)}, bf16[128,224]{1,0:T(8,128)(2,1)S(1)}, u32[]{:S(2)}, u32[]{:S(2)}) collective-permute-start(bf16[128,224]{1,0:T(8,128)(2,1)S(1)} %get-tuple-element.9), channel_id=1, source_target_pairs={{0,1},{1,0},{2,3},{3,2},{4,5},{5,4},{6,7},{7,6},{8,9},{9,8},{10,11... | collective-permute-start | bytes 172040 | tf_op jit(solution)/shard_map/ppermute | solution.py:25
  156.6 0.7 collective-permute-done.5
  157.4 0.7 broadcast_in_dim.161
  158.1 8.5 %all-to-all-start.3 = ((bf16[64,4,224]{2,1,0:T(4,128)(2,1)}), bf16[64,4,224]{2,1,0:T(4,128)(2,1)S(1)}, u32[]{:S(2)}, u32[]{:S(2)}) async-start(bf16[64,4,224]{2,1,0:T(4,128)(2,1)} %bitcast.20), calls=%async_computation.3 | async-start | bytes 262144 | tf_op jit(solution)/shard_map/all_to_all | solution.py:406
  166.7 8.7 %all-to-all-done.3 = bf16[64,4,224]{2,1,0:T(4,128)(2,1)S(1)} async-done(((bf16[64,4,224]{2,1,0:T(4,128)(2,1)}), bf16[64,4,224]{2,1,0:T(4,128)(2,1)S(1)}, u32[]{:S(2)}, u32[]{:S(2)}) %all-to-all-start.3) | async-done | bytes 114720 | tf_op jit(solution)/shard_map/all_to_all | solution.py:406
  175.5 0.7 add_convert_fusion.1.state_ref
  176.6 1.0 broadcast_in_dim.163
  177.6 4.9 %all-to-all-start.4 = ((bf16[64,2,1792]{2,1,0:T(2,128)(2,1)}), bf16[64,2,1792]{2,1,0:T(2,128)(2,1)S(1)}, u32[]{:S(2)}, u32[]{:S(2)}) async-start(bf16[64,2,1792]{2,1,0:T(2,128)(2,1)} %bitcast.24), calls=%async_computation.4 | async-start | bytes 917504 | tf_op jit(solution)/shard_map/all_to_all | solution.py:453
  183.1 10.0 %all-to-all-done.4 = bf16[64,2,1792]{2,1,0:T(2,128)(2,1)S(1)} async-done(((bf16[64,2,1792]{2,1,0:T(2,128)(2,1)}), bf16[64,2,1792]{2,1,0:T(2,128)(2,1)S(1)}, u32[]{:S(2)}, u32[]{:S(2)}) %all-to-all-start.4) | async-done | bytes 458784 | tf_op jit(solution)/shard_map/all_to_all | solution.py:453
  193.1 5.2 %all-gather.1 = bf16[128,2,1792]{2,1,0:T(2,128)(2,1)} all-gather(bf16[64,2,1792]{2,1,0:T(2,128)(2,1)S(1)} %all-to-all-done.4), channel_id=3, replica_groups=mesh['x_lo'=2,'z'=4,'y'=4,'x_hi'=2,'core'=2] {'core'}, dimensions={0}, use_global_device_ids=true | all-gather | bytes 1376256 | tf_op jit(solution)/shard_map/all_gather | solution.py:457
  198.3 10.5 %expert_inner.3 = bf16[64,512]{1,0:T(8,128)(2,1)} custom-call(bf16[2,64,2,1792]{3,2,1,0:T(2,128)(2,1)} %bitcast.100, f32[1,7168]{1,0:T(1,128)} %bitcast.115, bf16[7168,512]{1,0:T(8,128)(2,1)} %bitcast.94, bf16[7168,512]{1,0:T(8,128)(2,1)} %bitcast.97), custom_call_target="tpu_custom_call" | custom-call | flops 939524096 | bytes 14680064 | tf_op jit(solution)/shard_map/expert_inner/pallas_call | solution.py:249
  208.8 3.8 all-gather.2
  212.5 5.2 %expert_down.3 = bf16[64,3584]{1,0:T(8,128)(2,1)} custom-call(s32[1]{0:T(128)} %bitcast.10.core_ref, bf16[2,64,512]{2,1,0:T(8,128)(2,1)} %bitcast.107, bf16[512,7168]{1,0:T(8,128)(2,1)} %bitcast.91, bf16[512,3584]{1,0:T(8,128)(2,1)} %collective-permute-done.6.other_ref), custom_call_target="tpu_custom_call" | custom-call | flops 469762048 | bytes 7340032 | tf_op jit(solution)/shard_map/expert_down/pallas_call | solution.py:286
  217.8 1.1 reshape.326
  218.9 1.1 copy.52
  220.0 4.6 %all-to-all-start.5 = ((bf16[64,2,1792]{2,1,0:T(2,128)(2,1)}), bf16[64,2,1792]{2,1,0:T(2,128)(2,1)S(1)}, u32[]{:S(2)}, u32[]{:S(2)}) async-start(bf16[64,2,1792]{2,1,0:T(2,128)(2,1)} %bitcast.33), calls=%async_computation.5 | async-start | bytes 917504 | tf_op jit(solution)/shard_map/all_to_all | solution.py:470
  224.9 11.7 %all-to-all-done.5 = bf16[64,2,1792]{2,1,0:T(2,128)(2,1)S(1)} async-done(((bf16[64,2,1792]{2,1,0:T(2,128)(2,1)}), bf16[64,2,1792]{2,1,0:T(2,128)(2,1)S(1)}, u32[]{:S(2)}, u32[]{:S(2)}) %all-to-all-start.5) | async-done | bytes 458784 | tf_op jit(solution)/shard_map/all_to_all | solution.py:470
  236.8 0.5 collect_rows.3.state_ref
  237.9 15.0 %all_to_all.51 = bf16[64,2,1792]{2,1,0:T(2,128)(2,1)S(1)} all-to-all(bf16[64,2,1792]{2,1,0:T(2,128)(2,1)S(1)} %bitcast.106), channel_id=1, replica_groups=mesh['x_lo'=2,'z'=4,'y'=4,'x_hi'=2,'core'=2] {'x_lo','z','y','x_hi'}, dimensions={0} | all-to-all | bytes 917504 | tf_op jit(solution)/shard_map/all_to_all | solution.py:453
  252.9 5.2 %all-gather.3 = bf16[128,2,1792]{2,1,0:T(2,128)(2,1)} all-gather(bf16[64,2,1792]{2,1,0:T(2,128)(2,1)S(1)} %all_to_all.51), channel_id=5, replica_groups=mesh['x_lo'=2,'z'=4,'y'=4,'x_hi'=2,'core'=2] {'core'}, dimensions={0}, use_global_device_ids=true | all-gather | bytes 1376256 | tf_op jit(solution)/shard_map/all_gather | solution.py:457
  258.0 10.5 %expert_inner.4 = bf16[64,512]{1,0:T(8,128)(2,1)} custom-call(bf16[2,64,2,1792]{3,2,1,0:T(2,128)(2,1)} %bitcast.101, f32[1,7168]{1,0:T(1,128)} %bitcast.116, bf16[7168,512]{1,0:T(8,128)(2,1)} %bitcast.95, bf16[7168,512]{1,0:T(8,128)(2,1)} %bitcast.98), custom_call_target="tpu_custom_call" | custom-call | flops 939524096 | bytes 14680064 | tf_op jit(solution)/shard_map/expert_inner/pallas_call | solution.py:249
  268.5 3.6 all-gather.4
  272.1 5.2 %expert_down.4.after_ref = bf16[64,3584]{1,0:T(8,128)(2,1)} custom-call(s32[1]{0:T(128)} %bitcast.10.core_ref, bf16[2,64,512]{2,1,0:T(8,128)(2,1)} %bitcast.109, bf16[512,7168]{1,0:T(8,128)(2,1)} %bitcast.92, bf16[512,3584]{1,0:T(8,128)(2,1)} %collective-permute-done.6.other_ref), custom_call_target="tpu_custom_call" | custom-call | flops 469762048 | bytes 7340032 | tf_op jit(solution)/shard_map/expert_down/pallas_call | solution.py:286
  277.6 0.8 copy-done.8
  278.4 1.1 copy.54
  279.6 4.6 %all-to-all-start.7 = ((bf16[64,2,1792]{2,1,0:T(2,128)(2,1)}), bf16[64,2,1792]{2,1,0:T(2,128)(2,1)S(1)}, u32[]{:S(2)}, u32[]{:S(2)}) async-start(bf16[64,2,1792]{2,1,0:T(2,128)(2,1)} %bitcast.41), calls=%async_computation.7 | async-start | bytes 917504 | tf_op jit(solution)/shard_map/all_to_all | solution.py:470
  284.9 11.2 %all-to-all-done.7 = bf16[64,2,1792]{2,1,0:T(2,128)(2,1)S(1)} async-done(((bf16[64,2,1792]{2,1,0:T(2,128)(2,1)}), bf16[64,2,1792]{2,1,0:T(2,128)(2,1)S(1)}, u32[]{:S(2)}, u32[]{:S(2)}) %all-to-all-start.7) | async-done | bytes 458784 | tf_op jit(solution)/shard_map/all_to_all | solution.py:470
  296.3 0.5 collect_rows.4.rest_0_.state_ref
  297.2 1.0 broadcast_in_dim.173
  298.2 4.6 %all-to-all-start.8 = ((bf16[64,2,1792]{2,1,0:T(2,128)(2,1)}), bf16[64,2,1792]{2,1,0:T(2,128)(2,1)S(1)}, u32[]{:S(2)}, u32[]{:S(2)}) async-start(bf16[64,2,1792]{2,1,0:T(2,128)(2,1)} %bitcast.42), calls=%async_computation.8 | async-start | bytes 917504 | tf_op jit(solution)/shard_map/all_to_all | solution.py:453
  302.8 0.6 pad_maximum_fusion.1
  303.5 12.2 %prefill.2 = (bf16[512,512]{1,0:T(8,128)(2,1)}, f32[8,128]{1,0:T(8,128)}) custom-call(bf16[512,576]{1,0:T(8,128)(2,1)} %bitcast.127, bf16[32,576,128]{2,1,0:T(8,128)(2,1)} %tie.4.own_ref, bf16[32,576,128]{2,1,0:T(8,128)(2,1)} %collective-permute-done.7.other_ref, f32[8,1,1024]{2,1,0:T(1,128)} %bitcast.125, bf16[4,1792]{1,0:T(4,128)(2,1)} %copy-done.4), custom_call_target="tpu_custom_call" | custom-call | flops 4563402752 | bytes 9437184 | tf_op jit(solution)/shard_map/prefill/pallas_call | solution.py:179
  315.6 0.8 copy-done.7
  316.4 8.6 %all-gather.5 = bf16[128,2,1792]{2,1,0:T(2,128)(2,1)} all-gather(bf16[64,2,1792]{2,1,0:T(2,128)(2,1)} %tie.5), channel_id=7, replica_groups=mesh['x_lo'=2,'z'=4,'y'=4,'x_hi'=2,'core'=2] {'core'}, dimensions={0}, use_global_device_ids=true | all-gather | bytes 1376256 | tf_op jit(solution)/shard_map/all_gather | solution.py:457
  325.0 10.5 %expert_inner.5 = bf16[64,512]{1,0:T(8,128)(2,1)} custom-call(bf16[2,64,2,1792]{3,2,1,0:T(2,128)(2,1)} %bitcast.102, f32[1,7168]{1,0:T(1,128)} %bitcast.117, bf16[7168,512]{1,0:T(8,128)(2,1)} %bitcast.96, bf16[7168,512]{1,0:T(8,128)(2,1)} %bitcast.99), custom_call_target="tpu_custom_call" | custom-call | flops 939524096 | bytes 14680064 | tf_op jit(solution)/shard_map/expert_inner/pallas_call | solution.py:249
  335.5 3.4 all-gather.6
  338.9 5.2 %expert_down.5.rest_0_ = bf16[64,3584]{1,0:T(8,128)(2,1)} custom-call(s32[1]{0:T(128)} %bitcast.10.core_ref, bf16[2,64,512]{2,1,0:T(8,128)(2,1)} %bitcast.108, bf16[512,7168]{1,0:T(8,128)(2,1)} %bitcast.93, bf16[512,3584]{1,0:T(8,128)(2,1)} %collective-permute-done.6.other_ref), custom_call_target="tpu_custom_call" | custom-call | flops 469762048 | bytes 7340032 | tf_op jit(solution)/shard_map/expert_down/pallas_call | solution.py:286
  344.1 1.1 reshape.336
  345.3 1.1 copy.56
  346.4 9.9 %all-to-all-start.9 = ((bf16[64,2,1792]{2,1,0:T(2,128)(2,1)}), bf16[64,2,1792]{2,1,0:T(2,128)(2,1)S(1)}, u32[]{:S(2)}, u32[]{:S(2)}) async-start(bf16[64,2,1792]{2,1,0:T(2,128)(2,1)} %bitcast.49), calls=%async_computation.9 | async-start | bytes 917504 | tf_op jit(solution)/shard_map/all_to_all | solution.py:470
  356.4 12.2 %prefill.3 = (bf16[512,512]{1,0:T(8,128)(2,1)}, f32[8,128]{1,0:T(8,128)}) custom-call(bf16[512,576]{1,0:T(8,128)(2,1)} %bitcast.128, bf16[32,576,128]{2,1,0:T(8,128)(2,1)} %tie.4.own_ref, bf16[32,576,128]{2,1,0:T(8,128)(2,1)} %collective-permute-done.7.other_ref, f32[8,1,1024]{2,1,0:T(1,128)} %bitcast.126, ...), custom_call_target="tpu_custom_call", output_to_operand_aliasing={{0}: (5, {})} | custom-call | flops 4563402752 | bytes 9437184 | tf_op jit(solution)/shard_map/prefill/pallas_call | solution.py:179
  368.8 0.7 copy-done.6
  369.9 7.8 %all-gather.8 = bf16[4,4,1792]{2,1,0:T(4,128)(2,1)S(1)} all-gather(bf16[1,4,1792]{2,1,0:T(4,128)(2,1)S(1)} %bitcast.89), channel_id=9, replica_groups=mesh['x_lo'=2,'z'=4,'y'=4,'x_hi'=2,'core'=2] {'x_hi','core'}, dimensions={0}, use_global_device_ids=true | all-gather | bytes 71680 | tf_op jit(solution)/shard_map/all_gather | solution.py:473
  377.8 0.7 reshape.340
  (94 shorter events, 5.7 us)
Async XLA Ops:
  7.2 16.7 %copy-start.11 = (s32[32]{0:T(128)S(1)}, s32[32]{0:T(128)}, u32[]{:S(2)}) copy-start(s32[32]{0:T(128)} %param.16) | copy-start | bytes 388
  8.1 13.7 %collective-permute-start.1 = (bf16[576,128]{1,0:T(8,128)(2,1)S(1)}, bf16[576,128]{1,0:T(8,128)(2,1)S(1)}, u32[]{:S(2)}, u32[]{:S(2)}) collective-permute-start(bf16[576,128]{1,0:T(8,128)(2,1)S(1)} %get-tuple-element.17), channel_id=1, source_target_pairs={{0,12},{4,0},{8,4},{12,8},{1,13},{5,1},{9,5},{13,9},{2,14},{6,2},{... | collective-permute-start | bytes 442376 | tf_op jit(solution)/shard_map/ppermute | solution.py:25
  11.8 10.1 %collective-permute-start = (bf16[576,128]{1,0:T(8,128)(2,1)S(1)}, bf16[576,128]{1,0:T(8,128)(2,1)S(1)}, u32[]{:S(2)}, u32[]{:S(2)}) collective-permute-start(bf16[576,128]{1,0:T(8,128)(2,1)S(1)} %get-tuple-element.17), channel_id=1, source_target_pairs={{0,4},{4,8},{8,12},{12,0},{1,5},{5,9},{9,13},{13,1},{2,6},{6,10},{... | collective-permute-start | bytes 442376 | tf_op jit(solution)/shard_map/ppermute | solution.py:25
  11.8 10.1 %collective-permute-start.2 = (bf16[576,128]{1,0:T(8,128)(2,1)S(1)}, bf16[576,128]{1,0:T(8,128)(2,1)S(1)}, u32[]{:S(2)}, u32[]{:S(2)}) collective-permute-start(bf16[576,128]{1,0:T(8,128)(2,1)S(1)} %get-tuple-element.17), channel_id=1, source_target_pairs={{0,8},{4,12},{8,0},{12,4},{1,9},{5,13},{9,1},{13,5},{2,10},{6,14},... | collective-permute-start | bytes 442376 | tf_op jit(solution)/shard_map/ppermute | solution.py:25
  15.2 14.0 %all-to-all-start = ((bf16[8,64,576]{2,1,0:T(8,128)(2,1)}), bf16[8,64,576]{2,1,0:T(8,128)(2,1)S(1)}, u32[]{:S(2)}, u32[]{:S(2)}) async-start(bf16[8,64,576]{2,1,0:T(8,128)(2,1)} %broadcast_in_dim.148), calls=%async_computation | async-start | bytes 1310720 | tf_op jit(solution)/shard_map/all_to_all | solution.py:30
  21.2 256.2 %all-gather.11.cloned.1.call-start = ((), (), s32[]{:S(2)}) async-start(), calls=%async_computation.10 | async-start | bytes 5308416 | tf_op jit(solution)/shard_map/all_gather | solution.py:433
  22.0 25.0 %copy-start.1 = (bf16[4,576,128]{2,1,0:T(8,128)(2,1)}, bf16[4,576,128]{2,1,0:T(8,128)(2,1)S(1)}, u32[]{:S(2)}) copy-start(bf16[4,576,128]{2,1,0:T(8,128)(2,1)S(1)} %pad_maximum_fusion.own_ref.x_ref) | copy-start | bytes 1769476
  22.0 7.2 %collective-permute-start.3 = (bf16[4,576,128]{2,1,0:T(8,128)(2,1)S(1)}, bf16[4,576,128]{2,1,0:T(8,128)(2,1)S(1)}, u32[]{:S(2)}, u32[]{:S(2)}) collective-permute-start(bf16[4,576,128]{2,1,0:T(8,128)(2,1)S(1)} %pad_maximum_fusion.own_ref.x_ref), channel_id=1, source_target_pairs={{0,1},{1,0},{2,3},{3,2},{4,5},{5,4},{6,7},{7,6},{8,9},{9,8},{10,11... | collective-permute-start | bytes 1769480 | tf_op jit(solution)/shard_map/ppermute | solution.py:25
  47.0 0.6 copy-start.2
  50.5 95.1 %collective-permute-start.4 = (bf16[8,224,512]{2,1,0:T(8,128)(2,1)}, bf16[8,224,512]{2,1,0:T(8,128)(2,1)S(1)}, u32[]{:S(2)}, u32[]{:S(2)}) collective-permute-start(bf16[8,224,512]{2,1,0:T(8,128)(2,1)} %dynamic-slice_bitcast_fusion.1), channel_id=1, source_target_pairs={{0,64},{64,0},{1,65},{65,1},{2,66},{66,2},{3,67},{67,3},{4,68},{68... | collective-permute-start | bytes 5505032 | tf_op jit(solution)/shard_map/ppermute | solution.py:25
  50.5 7.2 %copy-start.3 = (bf16[64,512]{1,0:T(8,128)(2,1)S(1)}, bf16[64,512]{1,0:T(8,128)(2,1)}, u32[]{:S(2)}) copy-start(bf16[64,512]{1,0:T(8,128)(2,1)} %copy-done.2) | copy-start | bytes 196612
  50.5 13.7 %copy-start.9 = (s32[3,4,8]{2,1,0:T(4,128)S(1)}, s32[3,4,8]{2,1,0:T(4,128)}, u32[]{:S(2)}) copy-start(s32[3,4,8]{2,1,0:T(4,128)} %param.24) | copy-start | bytes 1156
  54.6 157.9 %collective-permute-start.6 = (bf16[512,3584]{1,0:T(8,128)(2,1)}, bf16[512,3584]{1,0:T(8,128)(2,1)}, u32[]{:S(2)}, u32[]{:S(2)}) collective-permute-start(bf16[512,3584]{1,0:T(8,128)(2,1)} %dynamic-slice_bitcast_fusion), channel_id=1, source_target_pairs={{0,1},{1,0},{2,3},{3,2},{4,5},{5,4},{6,7},{7,6},{8,9},{9,8},{10,11... | collective-permute-start | bytes 11010056 | tf_op jit(solution)/shard_map/ppermute | solution.py:25
  59.3 84.9 %all-to-all-start.2 = ((bf16[32,4,4096]{2,1,0:T(4,128)(2,1)}), bf16[32,4,4096]{2,1,0:T(4,128)(2,1)}, u32[]{:S(2)}, u32[]{:S(2)}) async-start(bf16[32,4,4096]{2,1,0:T(4,128)(2,1)} %bitcast.17), calls=%async_computation.2 | async-start | bytes 2097152 | tf_op jit(solution)/shard_map/all_to_all | solution.py:396
  145.6 2.0 copy-start
  147.7 35.0 %copy-start.10 = (f32[3,4,8]{2,1,0:T(4,128)S(1)}, f32[3,4,8]{2,1,0:T(4,128)}, u32[]{:S(2)}) copy-start(f32[3,4,8]{2,1,0:T(4,128)} %param.25) | copy-start | bytes 1156
  149.6 7.8 %collective-permute-start.5 = (bf16[128,224]{1,0:T(8,128)(2,1)S(1)}, bf16[128,224]{1,0:T(8,128)(2,1)S(1)}, u32[]{:S(2)}, u32[]{:S(2)}) collective-permute-start(bf16[128,224]{1,0:T(8,128)(2,1)S(1)} %get-tuple-element.9), channel_id=1, source_target_pairs={{0,1},{1,0},{2,3},{3,2},{4,5},{5,4},{6,7},{7,6},{8,9},{9,8},{10,11... | collective-permute-start | bytes 172040 | tf_op jit(solution)/shard_map/ppermute | solution.py:25
  158.1 17.3 %all-to-all-start.3 = ((bf16[64,4,224]{2,1,0:T(4,128)(2,1)}), bf16[64,4,224]{2,1,0:T(4,128)(2,1)S(1)}, u32[]{:S(2)}, u32[]{:S(2)}) async-start(bf16[64,4,224]{2,1,0:T(4,128)(2,1)} %bitcast.20), calls=%async_computation.3 | async-start | bytes 262144 | tf_op jit(solution)/shard_map/all_to_all | solution.py:406
  177.6 15.5 %all-to-all-start.4 = ((bf16[64,2,1792]{2,1,0:T(2,128)(2,1)}), bf16[64,2,1792]{2,1,0:T(2,128)(2,1)S(1)}, u32[]{:S(2)}, u32[]{:S(2)}) async-start(bf16[64,2,1792]{2,1,0:T(2,128)(2,1)} %bitcast.24), calls=%async_computation.4 | async-start | bytes 917504 | tf_op jit(solution)/shard_map/all_to_all | solution.py:453
  220.0 16.6 %all-to-all-start.5 = ((bf16[64,2,1792]{2,1,0:T(2,128)(2,1)}), bf16[64,2,1792]{2,1,0:T(2,128)(2,1)S(1)}, u32[]{:S(2)}, u32[]{:S(2)}) async-start(bf16[64,2,1792]{2,1,0:T(2,128)(2,1)} %bitcast.33), calls=%async_computation.5 | async-start | bytes 917504 | tf_op jit(solution)/shard_map/all_to_all | solution.py:470
  277.3 1.0 copy-start.8
  277.3 26.1 %collective-permute-start.7 = (bf16[32,576,128]{2,1,0:T(8,128)(2,1)}, bf16[32,576,128]{2,1,0:T(8,128)(2,1)}, u32[]{:S(2)}, u32[]{:S(2)}) collective-permute-start(bf16[32,576,128]{2,1,0:T(8,128)(2,1)} %tie.4.own_ref), channel_id=1, source_target_pairs={{0,1},{1,0},{2,3},{3,2},{4,5},{5,4},{6,7},{7,6},{8,9},{9,8},{10,11... | collective-permute-start | bytes 14155784 | tf_op jit(solution)/shard_map/ppermute | solution.py:25
  279.6 16.6 %all-to-all-start.7 = ((bf16[64,2,1792]{2,1,0:T(2,128)(2,1)}), bf16[64,2,1792]{2,1,0:T(2,128)(2,1)S(1)}, u32[]{:S(2)}, u32[]{:S(2)}) async-start(bf16[64,2,1792]{2,1,0:T(2,128)(2,1)} %bitcast.41), calls=%async_computation.7 | async-start | bytes 917504 | tf_op jit(solution)/shard_map/all_to_all | solution.py:470
  296.8 6.7 %copy-start.4 = (bf16[4,1792]{1,0:T(4,128)(2,1)}, bf16[4,1792]{1,0:T(4,128)(2,1)S(1)}, u32[]{:S(2)}) copy-start(bf16[4,1792]{1,0:T(4,128)(2,1)S(1)} %collect_rows.4.rest_0_.state_ref) | copy-start | bytes 43012
  298.2 17.4 %all-to-all-start.8 = ((bf16[64,2,1792]{2,1,0:T(2,128)(2,1)}), bf16[64,2,1792]{2,1,0:T(2,128)(2,1)S(1)}, u32[]{:S(2)}, u32[]{:S(2)}) async-start(bf16[64,2,1792]{2,1,0:T(2,128)(2,1)} %bitcast.42), calls=%async_computation.8 | async-start | bytes 917504 | tf_op jit(solution)/shard_map/all_to_all | solution.py:453
  315.6 0.8 copy-start.7
  346.4 22.2 %all-to-all-start.9 = ((bf16[64,2,1792]{2,1,0:T(2,128)(2,1)}), bf16[64,2,1792]{2,1,0:T(2,128)(2,1)S(1)}, u32[]{:S(2)}, u32[]{:S(2)}) async-start(bf16[64,2,1792]{2,1,0:T(2,128)(2,1)} %bitcast.49), calls=%async_computation.9 | async-start | bytes 917504 | tf_op jit(solution)/shard_map/all_to_all | solution.py:470
  356.4 12.4 %copy-start.5 = (bf16[4,1792]{1,0:T(4,128)(2,1)S(1)}, bf16[4,1792]{1,0:T(4,128)(2,1)}, u32[]{:S(2)}) copy-start(bf16[4,1792]{1,0:T(4,128)(2,1)} %copy-done.4) | copy-start | bytes 43012
  368.8 0.7 copy-start.6
Sparse Core Ops, SparseCore 0:
  47.8 100.6 all-gather.10
